TPU v7x, 128 devices: a whole 4x4x4 slice. The times are simulated.
128 devices in a mesh: outer: 16 (over z, y), narrow: 8 (over x, core).
Axes of the slice: x: 4, y: 4, z: 4, core: 2. Of those that a mesh axis runs over, the one named last changes fastest.
Arguments:
- queries: bfloat16 [32768, 4096], P(('outer', 'narrow')), may hold values from -6 to 6
- keys: bfloat16 [32768, 4096], P(('outer', 'narrow')), may hold values from -6 to 6
- values: bfloat16 [32768, 4096], P(('outer', 'narrow')), may hold values from -6 to 6
- log_decay: float32 [32, 32768], P(None, ('outer', 'narrow')), may hold values from -0.8 to 0
- gain: float32 [4096], replicated, may hold values from 0.5 to 1.5
Outputs:
- mixed: bfloat16 [32768, 4096], P(('outer', 'narrow'))
All inputs are finite; a program needn't handle non-finite values.
Results may differ from a plain program's by a relative error of at most 0.0052.
Values may be sent and summed in bfloat16 or wider, within the bound.
No kernel may reach another device: no remote copies, remote signals or barrier semaphores. Data moves between devices by JAX's collectives and lax.ppermute only.
A program may use at most 64 MiB of HBM per device.

v0:
```python
import math

import jax
import jax.numpy as jnp
from jax import lax
from jax.sharding import Mesh
from jax.sharding import PartitionSpec as P

OUTER = ("outer_0", "outer_1")
OUTER_NARROW = ("outer_0", "outer_1", "narrow")


def nothing_yet(shard, identity):
    return jax.tree.map(
        lambda a, e: jnp.broadcast_to(jnp.asarray(e, a.dtype), a.shape), shard, identity
    )


def carried_in(shard, axes, combine, identity):
    before = start = nothing_yet(shard, identity)
    running = shard
    for axis in reversed(axes):
        devices, position = (lax.axis_size(axis), lax.axis_index(axis))
        pieces = jax.tree.map(lambda part: lax.all_gather(part, axis), running)
        inside, running = (start, start)
        for k in range(devices):
            passed = k < position
            running = combine(running, jax.tree.map(lambda part: part[k], pieces))
            inside = jax.tree.map(lambda new, old: jnp.where(passed, new, old), running, inside)
        before = combine(inside, before)
    return before


def combine(earlier, later):
    return (earlier[0] + later[0], jnp.exp(later[0])[:, None, None] * earlier[1] + later[1])


def group_prefix(totals, states):
    start = (jnp.zeros(totals.shape[1:], jnp.float32), jnp.zeros(states.shape[1:], jnp.float32))

    def advance(carry, item):
        return (combine(carry, item), carry)

    whole, before = lax.scan(advance, start, (totals, states))
    return (whole, before)


def on_device(queries, keys, values, log_decay, gain):
    tokens = queries.shape[0]
    heads = log_decay.shape[0]
    width = queries.shape[1] // heads
    qthree = queries.reshape(tokens, heads, width)
    kthree = keys.reshape(tokens, heads, width)
    vthree = values.reshape(tokens, heads, width)
    cum = jnp.cumsum(log_decay, axis=1)
    total = cum[:, -1]
    factor = jnp.exp(total[:, None] - cum).T
    decayed = (kthree.astype(jnp.float32) * factor[:, :, None]).astype(jnp.bfloat16)
    block_state = jnp.einsum("thd,the->hde", decayed, vthree, preferred_element_type=jnp.float32)
    moved_states, moved_totals = (
        lax.all_to_all(block_state[None], "narrow", split_axis=1, concat_axis=0, tiled=True),
        lax.all_to_all(total[None], "narrow", split_axis=1, concat_axis=0, tiled=True),
    )
    whole, before = group_prefix(moved_totals, moved_states)
    owned = moved_totals.shape[1]
    identity = (jnp.zeros((owned,), jnp.float32), jnp.zeros((owned, width, width), jnp.float32))
    earlier = carried_in(whole, OUTER, combine, identity)
    prefix = jnp.exp(before[0])[:, :, None, None] * earlier[1][None] + before[1]
    back = lax.all_to_all(
        prefix.astype(jnp.bfloat16), "narrow", split_axis=0, concat_axis=1, tiled=True
    )
    carried_half = back.reshape(heads, width, width)
    causal = jnp.arange(tokens)[:, None] >= jnp.arange(tokens)[None, :]
    group = math.gcd(heads, 8)
    pieces = []
    for first in range(0, heads, group):
        qpart = qthree[:, first : first + group]
        kpart = kthree[:, first : first + group]
        vpart = vthree[:, first : first + group]
        running_partial = cum[first : first + group]
        scores = jnp.einsum("thd,shd->hts", qpart, kpart, preferred_element_type=jnp.float32)
        spread = jnp.minimum(running_partial[:, :, None] - running_partial[:, None, :], 0.0)
        weights = jnp.where(causal[None], scores * jnp.exp(spread), 0.0).astype(jnp.bfloat16)
        inner = jnp.einsum("hts,she->the", weights, vpart, preferred_element_type=jnp.float32)
        readout = jnp.einsum(
            "thd,hde->the",
            qpart,
            carried_half[first : first + group],
            preferred_element_type=jnp.float32,
        )
        pieces.append(inner + readout * jnp.exp(running_partial).T[:, :, None])
    numer = jnp.concatenate(pieces, axis=1)
    scale = lax.rsqrt(jnp.mean(numer * numer, axis=-1, keepdims=True) + 1e-06)
    result = numer * scale * gain.reshape(heads, width)[None]
    return result.astype(jnp.bfloat16).reshape(tokens, heads * width)


def solution(mesh):
    split = Mesh(mesh.devices.reshape(4, 4, mesh.shape["narrow"]), ("outer_0", "outer_1", "narrow"))
    placed = (
        P(OUTER_NARROW, None),
        P(OUTER_NARROW, None),
        P(OUTER_NARROW, None),
        P(None, OUTER_NARROW),
        P(),
    )
    return jax.shard_map(
        on_device, mesh=split, in_specs=placed, out_specs=P(OUTER_NARROW, None), check_vma=False
    )
```

profile of v0, /device:TPU:1, one launch (start us, length us, event | category | flops | bytes accessed | tf_op | source)
XLA Modules:
  0.0 171.0 jit_solution(5586449919091520039)
XLA Ops:
  6.5 0.8 copy-done
  8.3 0.7 all_to_all.13
  9.0 5.8 %all-to-all-start = ((f32[1,8,4]{2,0,1:T(1,128)}), f32[1,8,4]{2,0,1:T(1,128)S(1)}, u32[]{:S(2)}, u32[]{:S(2)}) async-start(f32[1,8,4]{2,0,1:T(1,128)} %bitcast.5), calls=%async_computation | async-start | bytes 8192 | tf_op jit(solution)/shard_map/all_to_all | solution.py:62
  14.9 4.1 %copy.75 = bf16[256,4096]{0,1:T(8,128)(2,1)} copy(bf16[256,4096]{1,0:T(8,128)(2,1)} %param.8) | data formatting | bytes 4194304 | tf_op args[1]
  19.0 3.3 %copy.78 = bf16[256,4096]{0,1:T(8,128)(2,1)S(1)} copy(bf16[256,4096]{1,0:T(8,128)(2,1)} %param.9) | data formatting | bytes 4194304 | tf_op args[2]
  22.3 3.6 %fusion.7 = f32[1,32,128,128]{3,2,0,1:T(8,128)} fusion(bf16[256,32,128]{0,2,1:T(8,128)(2,1)S(1)} %bitcast.174, bf16[256,32,128]{0,2,1:T(8,128)(2,1)} %bitcast.180, f32[256,32]{0,1:T(8,128)S(1)} %exponential_bitcast_fusion), kind=kOutput, calls=%fused_computation.20 | convolution fusion | flops 271581184 | bytes 6324224 | tf_op jit(solution)/shard_map/thd,the->hde/dot_general | solution.py:59
  25.9 4.8 %all-to-all-start.1 = ((f32[1,32,128,128]{3,2,0,1:T(8,128)}), f32[1,32,128,128]{3,2,0,1:T(8,128)}, u32[]{:S(2)}, u32[]{:S(2)}) async-start(f32[1,32,128,128]{3,2,0,1:T(8,128)} %fusion.7), calls=%async_computation.1 | async-start | bytes 4194304 | tf_op jit(solution)/shard_map/all_to_all | solution.py:61
  30.7 26.4 %all-to-all-done.1 = f32[1,32,128,128]{3,2,0,1:T(8,128)} async-done(((f32[1,32,128,128]{3,2,0,1:T(8,128)}), f32[1,32,128,128]{3,2,0,1:T(8,128)}, u32[]{:S(2)}, u32[]{:S(2)}) %all-to-all-start.1) | async-done | bytes 2097184 | tf_op jit(solution)/shard_map/all_to_all | solution.py:61
  57.2 14.8 %while.17 = (s32[]{:T(128)}, f32[4]{0:T(128)S(1)}, f32[4,128,128]{2,1,0:T(8,128)S(1)}, f32[8,4]{1,0:T(8,128)S(1)}, f32[8,4,128,128]{3,2,1,0:T(8,128)}, /*index=5...) while((s32[]{:T(128)}, f32[4]{0:T(128)S(1)}, ...), condition=%wide.region_3.4_spmd.clone, body=%wide.region_2.3_spmd.clone.sunk | while | flops 262155 | bytes 1311477 | solution.py:44
  57.2 0.7 bitcast_dynamic-update-slice_fusion.2
  57.9 1.0 bitcast_add_fusion.2
  59.0 0.7 bitcast_dynamic-update-slice_fusion.2
  59.7 1.0 bitcast_add_fusion.2
  60.9 0.7 bitcast_dynamic-update-slice_fusion.2
  61.6 1.0 bitcast_add_fusion.2
  62.7 0.7 bitcast_dynamic-update-slice_fusion.2
  63.5 1.0 bitcast_add_fusion.2
  64.6 0.7 bitcast_dynamic-update-slice_fusion.2
  65.3 1.0 bitcast_add_fusion.2
  66.4 0.7 bitcast_dynamic-update-slice_fusion.2
  67.2 1.0 bitcast_add_fusion.2
  68.3 0.7 bitcast_dynamic-update-slice_fusion.2
  69.1 1.0 bitcast_add_fusion.2
  70.2 0.7 bitcast_dynamic-update-slice_fusion.2
  70.9 1.0 bitcast_add_fusion.2
  72.0 0.7 copy-done.1
  72.8 4.1 %copy.73 = bf16[256,4096]{0,1:T(8,128)(2,1)} copy(bf16[256,4096]{1,0:T(8,128)(2,1)} %param.7) | data formatting | bytes 4194304 | tf_op args[0]
  78.6 8.7 %all-reduce = f32[16]{0:T(128)S(1)} all-reduce(f32[16]{0:T(128)S(1)} %dynamic-update-slice), channel_id=2, replica_groups=mesh['outer_0'=4,'outer_1'=4,'narrow'=8] {'outer_1'}, use_global_device_ids=true, to_apply=%add | all-reduce | flops 16 | bytes 128
  87.4 9.4 %all-gather.8.cloned.1.call-done = f32[16,128,128]{2,1,0:T(8,128)} async-done(((f32[4,128,128]{2,1,0:T(8,128)}), f32[16,128,128]{2,1,0:T(8,128)}) %all-gather.8.cloned.1.call-update) | async-done | bytes 1048592 | tf_op jit(solution)/shard_map/all_gather | solution.py:24
  96.8 2.0 %fusion.32 = f32[1,4,128,128]{3,2,1,0:T(8,128)} fusion(f32[16,128,128]{2,1,0:T(8,128)} %all-gather.8.cloned.1.call-done, f32[4]{0:T(128)S(1)} %get-tuple-element.146, f32[4]{0:T(128)S(1)} %get-tuple-element.147, f32[4]{0:T(128)S(1)} %get-tuple-element.145, f32[4]{0:T(128)S(1)} %get-tuple-element.144), kind=kLoop, calls=%fused_computation.58 | loop fusion | flops 458752 | bytes 1310784 | tf_op jit(solution)/shard_map/add | solution.py:35
  98.8 2.0 %select_convert_fusion.3 = bf16[8,256,256]{2,1,0:T(8,128)(2,1)S(1)} fusion(bf16[256,32,128]{0,2,1:T(8,128)(2,1)} %bitcast.185, f32[8,256]{1,0:T(8,128)S(1)} %get-tuple-element.135, pred[256,256]{1,0:T(8,128)(4,1)S(1)} %iota_compare_fusion, bf16[256,32,128]{0,2,1:T(8,128)(2,1)} %bitcast.181), kind=kOutput, calls=%fused_computation.19 | convolution fusion | flops 136839168 | bytes 3751936 | tf_op jit(solution)/shard_map/thd,shd->hts/dot_general | solution.py:81
  100.9 1.5 convolution_bitcast_fusion.7
  102.8 1.8 %select_convert_fusion.2 = bf16[8,256,256]{2,1,0:T(8,128)(2,1)S(1)} fusion(bf16[256,32,128]{0,2,1:T(8,128)(2,1)} %bitcast.186, f32[8,256]{1,0:T(8,128)S(1)} %get-tuple-element.138, pred[256,256]{1,0:T(8,128)(4,1)S(1)} %iota_compare_fusion, bf16[256,32,128]{0,2,1:T(8,128)(2,1)S(1)} %bitcast.183), kind=kOutput, calls=%fused_computation.16 | convolution fusion | flops 136839168 | bytes 3751936 | tf_op jit(solution)/shard_map/thd,shd->hts/dot_general | solution.py:81
  104.6 1.5 convolution_bitcast_fusion.6
  106.5 1.8 %select_convert_fusion.1 = bf16[8,256,256]{2,1,0:T(8,128)(2,1)} fusion(bf16[256,32,128]{0,2,1:T(8,128)(2,1)S(1)} %bitcast.188, f32[8,256]{1,0:T(8,128)S(1)} %get-tuple-element.137, pred[256,256]{1,0:T(8,128)(4,1)S(1)} %iota_compare_fusion, bf16[256,32,128]{0,2,1:T(8,128)(2,1)S(1)} %bitcast.184), kind=kOutput, calls=%fused_computation.15 | convolution fusion | flops 136839168 | bytes 3751936 | tf_op jit(solution)/shard_map/thd,shd->hts/dot_general | solution.py:81
  108.3 8.5 %all-gather.2 = f32[4,1,4]{2,1,0:T(1,128)S(1)} all-gather(f32[1,1,4]{2,1,0:T(1,128)S(1)} %get-tuple-element.122), channel_id=1, replica_groups=mesh['outer_0'=4,'outer_1'=4,'narrow'=8] {'outer_0'}, dimensions={0}, use_global_device_ids=true | all-gather | bytes 80 | tf_op jit(solution)/shard_map/all_gather | solution.py:24
  116.9 6.6 %all-gather.6.cloned.1.call-done = f32[4,4,128,128]{3,2,1,0:T(8,128)} async-done(((f32[1,4,128,128]{3,2,1,0:T(8,128)}), f32[4,4,128,128]{3,2,1,0:T(8,128)}) %all-gather.6.cloned.1.call-update) | async-done | bytes 1048592 | tf_op jit(solution)/shard_map/all_gather | solution.py:24
  123.5 1.7 %fusion.31 = f32[4,128,128]{2,1,0:T(8,128)S(1)} fusion(f32[4,4,128,128]{3,2,1,0:T(8,128)} %all-gather.6.cloned.1.call-done, f32[16,128,128]{2,1,0:T(8,128)S(1)} %copy-done.6, f32[4]{0:T(128)S(1)} %get-tuple-element.143, f32[4]{0:T(128)S(1)} %get-tuple-element.145, f32[4]{0:T(128)S(1)} %get-tuple-element.147, f32[4]{0:T(128)S(1)} %get-tuple-element.142, ...), kind=kLoop, calls=%fused_computation.53 | loop fusion | flops 1572864 | bytes 2359448 | tf_op jit(solution)/shard_map/mul | solution.py:68
  125.4 1.3 add_convert_fusion
  126.7 5.8 %all-to-all-start.2 = ((bf16[8,4,128,128]{3,2,1,0:T(8,128)(2,1)}), bf16[8,4,128,128]{3,2,1,0:T(8,128)(2,1)S(1)}, u32[]{:S(2)}, u32[]{:S(2)}) async-start(bf16[8,4,128,128]{3,2,1,0:T(8,128)(2,1)} %add_convert_fusion), calls=%async_computation.2 | async-start | bytes 2097152 | tf_op jit(solution)/shard_map/all_to_all | solution.py:69
  132.5 2.8 %convolution_bitcast_fusion.5 = f32[256,8,128]{0,2,1:T(8,128)} fusion(bf16[8,256,256]{2,1,0:T(8,128)(2,1)} %select_convert_fusion.1, bf16[256,32,128]{0,2,1:T(8,128)(2,1)S(1)} %bitcast.177), kind=kOutput, calls=%fused_computation.34 | convolution fusion | flops 134217728 | bytes 2621440 | tf_op jit(solution)/shard_map/hts,she->the/dot_general | solution.py:84
  135.4 1.8 %select_convert_fusion = bf16[8,256,256]{2,1,0:T(8,128)(2,1)S(1)} fusion(bf16[256,32,128]{0,2,1:T(8,128)(2,1)S(1)} %bitcast.189, f32[8,256]{1,0:T(8,128)S(1)} %get-tuple-element.136, pred[256,256]{1,0:T(8,128)(4,1)S(1)} %iota_compare_fusion, bf16[256,32,128]{0,2,1:T(8,128)(2,1)} %bitcast.182), kind=kOutput, calls=%fused_computation.14 | convolution fusion | flops 136839168 | bytes 3751936 | tf_op jit(solution)/shard_map/thd,shd->hts/dot_general | solution.py:81
  137.2 1.5 convolution_bitcast_fusion.4
  138.7 8.9 %all-to-all-done.2 = bf16[8,4,128,128]{3,2,1,0:T(8,128)(2,1)S(1)} async-done(((bf16[8,4,128,128]{3,2,1,0:T(8,128)(2,1)}), bf16[8,4,128,128]{3,2,1,0:T(8,128)(2,1)S(1)}, u32[]{:S(2)}, u32[]{:S(2)}) %all-to-all-start.2) | async-done | bytes 1048608 | tf_op jit(solution)/shard_map/all_to_all | solution.py:69
  147.7 1.5 fusion.15
  152.1 2.5 %fusion.4 = f32[256,32,128]{0,2,1:T(8,128)} fusion(f32[256,8,128]{0,2,1:T(8,128)S(1)} %fusion.9, f32[256,8,128]{0,2,1:T(8,128)S(1)} %fusion.11, f32[256,8,128]{0,2,1:T(8,128)S(1)} %fusion.13, f32[256,8,128]{0,2,1:T(8,128)S(1)} %fusion.15, f32[256,32]{0,1:T(8,128)S(1)} %add_rsqrt_fusion), kind=kLoop, calls=%fused_computation.12 | loop fusion | flops 4194304 | bytes 8421376 | tf_op jit(solution)/shard_map/mul | solution.py:94
  154.6 5.7 %copy.95 = f32[256,4096]{1,0:T(8,128)} copy(f32[256,4096]{0,1:T(8,128)} %bitcast.179) | data formatting | bytes 8388608 | tf_op jit(solution)/shard_map/mul | solution.py:94
  160.3 3.9 %multiply_convert_fusion = bf16[256,4096]{1,0:T(8,128)(2,1)} fusion(f32[256,4096]{1,0:T(8,128)} %copy.95, f32[4096]{0:T(1024)S(1)} %copy-done.12), kind=kLoop, calls=%fused_computation.9 | loop fusion | flops 2097152 | bytes 6307840 | tf_op jit(solution)/shard_map/convert_element_type | solution.py:95
  (76 shorter events, 6.7 us)
Async XLA Ops:
  6.5 0.8 copy-start
  9.0 16.9 %all-to-all-start = ((f32[1,8,4]{2,0,1:T(1,128)}), f32[1,8,4]{2,0,1:T(1,128)S(1)}, u32[]{:S(2)}, u32[]{:S(2)}) async-start(f32[1,8,4]{2,0,1:T(1,128)} %bitcast.5), calls=%async_computation | async-start | bytes 8192 | tf_op jit(solution)/shard_map/all_to_all | solution.py:62
  25.9 31.2 %all-to-all-start.1 = ((f32[1,32,128,128]{3,2,0,1:T(8,128)}), f32[1,32,128,128]{3,2,0,1:T(8,128)}, u32[]{:S(2)}, u32[]{:S(2)}) async-start(f32[1,32,128,128]{3,2,0,1:T(8,128)} %fusion.7), calls=%async_computation.1 | async-start | bytes 4194304 | tf_op jit(solution)/shard_map/all_to_all | solution.py:61
  30.7 66.1 %all-gather.8.cloned.1.call-start = ((), (), s32[]{:S(2)}) async-start(), calls=%async_computation.4 | async-start | bytes 1310720 | tf_op jit(solution)/shard_map/all_gather | solution.py:24
  72.0 0.7 copy-start.1
  72.7 50.7 %all-gather.6.cloned.1.call-start = ((), (), s32[]{:S(2)}) async-start(), calls=%async_computation.3 | async-start | bytes 1310720 | tf_op jit(solution)/shard_map/all_gather | solution.py:24
  72.8 4.1 %copy-start.13 = (u32[128]{0:T(128)S(1)}, u32[128]{0:T(128)}, u32[]{:S(2)}) copy-start(u32[128]{0:T(128)} %constant.47) | copy-start | bytes 1540
  100.9 1.9 %copy-start.2 = (bf16[256,4096]{0,1:T(8,128)(2,1)S(1)}, bf16[256,4096]{0,1:T(8,128)(2,1)}, u32[]{:S(2)}) copy-start(bf16[256,4096]{0,1:T(8,128)(2,1)} %copy.75) | copy-start | bytes 6291460
  104.6 1.9 %copy-start.3 = (bf16[256,4096]{0,1:T(8,128)(2,1)S(1)}, bf16[256,4096]{0,1:T(8,128)(2,1)}, u32[]{:S(2)}) copy-start(bf16[256,4096]{0,1:T(8,128)(2,1)} %copy.73) | copy-start | bytes 6291460
  106.5 16.9 %copy-start.6 = (f32[16,128,128]{2,1,0:T(8,128)S(1)}, f32[16,128,128]{2,1,0:T(8,128)}, u32[]{:S(2)}) copy-start(f32[16,128,128]{2,1,0:T(8,128)} %all-gather.8.cloned.1.call-done) | copy-start | bytes 3145732
  123.4 1.9 %copy-start.11 = (f32[8,4,128,128]{3,2,1,0:T(8,128)S(1)}, f32[8,4,128,128]{3,2,1,0:T(8,128)}, u32[]{:S(2)}) copy-start(f32[8,4,128,128]{3,2,1,0:T(8,128)} %get-tuple-element.48) | copy-start | bytes 6291460
  126.7 20.9 %all-to-all-start.2 = ((bf16[8,4,128,128]{3,2,1,0:T(8,128)(2,1)}), bf16[8,4,128,128]{3,2,1,0:T(8,128)(2,1)S(1)}, u32[]{:S(2)}, u32[]{:S(2)}) async-start(bf16[8,4,128,128]{3,2,1,0:T(8,128)(2,1)} %add_convert_fusion), calls=%async_computation.2 | async-start | bytes 2097152 | tf_op jit(solution)/shard_map/all_to_all | solution.py:69
  132.5 2.9 %copy-start.4 = (bf16[256,4096]{0,1:T(8,128)(2,1)S(1)}, bf16[256,4096]{0,1:T(8,128)(2,1)}, u32[]{:S(2)}) copy-start(bf16[256,4096]{0,1:T(8,128)(2,1)} %copy.73) | copy-start | bytes 6291460
  138.7 9.0 %copy-start.7 = (f32[256,8,128]{0,2,1:T(8,128)S(1)}, f32[256,8,128]{0,2,1:T(8,128)}, u32[]{:S(2)}) copy-start(f32[256,8,128]{0,2,1:T(8,128)} %convolution_bitcast_fusion.7) | copy-start | bytes 3145732
  147.6 1.7 %copy-start.5 = (bf16[256,4096]{0,1:T(8,128)(2,1)S(1)}, bf16[256,4096]{0,1:T(8,128)(2,1)}, u32[]{:S(2)}) copy-start(bf16[256,4096]{0,1:T(8,128)(2,1)} %copy.73) | copy-start | bytes 6291460
  147.6 2.0 %copy-start.8 = (f32[256,8,128]{0,2,1:T(8,128)S(1)}, f32[256,8,128]{0,2,1:T(8,128)}, u32[]{:S(2)}) copy-start(f32[256,8,128]{0,2,1:T(8,128)} %convolution_bitcast_fusion.6) | copy-start | bytes 3145732
  149.3 1.3 copy-start.9
  150.0 1.3 copy-start.10
  154.6 5.7 %copy-start.12 = (f32[4096]{0:T(1024)S(1)}, f32[4096]{0:T(1024)}, u32[]{:S(2)}) copy-start(f32[4096]{0:T(1024)} %param.11) | copy-start | bytes 49156
Sparse Core Ops, SparseCore 0:
  72.9 23.8 all-gather.7
  99.0 24.4 all-gather.5
where the time goes:
time: 172 us; the launch traced here: 171 us
  waiting for transfers between devices  51.3 us (30%)
  other arithmetic  27.3 us (16%)
  local copies, waits for them, and re-layouts  23.2 us (13%)
  matrix products  21 us (12%)
  blocking collectives  17.2 us (10%)
  starting transfers between devices  16.5 us (10%)
  between operations  14.3 us (8%)
    all_to_all x1, waiting for transfers between devices, on_device(): lax.all_to_all(block_state[None], 'narrow', split_axis=1, concat_axis=0,...  26.4 us
    unnamed x34, local copies, waits for them, and re-layouts  16.1 us
    all_gather x2, waiting for transfers between devices, carried_in(): pieces = jax.tree.map(lambda part: lax.all_gather(part, axis), running)  15.9 us
    add x9, other arithmetic, combine(): jnp.exp(later[0])[:, None, None] * earlier[1] + later[1]  10.4 us
    all_to_all x1, waiting for transfers between devices, on_device(): lax.all_to_all(prefix.astype(jnp.bfloat16), 'narrow', split_axis=0, conca...  8.93 us
    unnamed x1, blocking collectives  8.7 us
    all_gather x1, blocking collectives, carried_in(): pieces = jax.tree.map(lambda part: lax.all_gather(part, axis), running)  8.53 us
    dot_general x4, matrix products, on_device(): jnp.einsum('thd,shd->hts', qpart, kpart, preferred_element_type=jnp.float32)  7.51 us
  transfers between devices with their start and end apart: 5, of which 4 were waited for; matrix products, arithmetic and copies ran while one was open for 18% of the time, Pallas kernels for 0%

commit v1 on v0

v1 whole, which is shorter than its diff:
```python
import functools

import jax
import jax.numpy as jnp
from jax import lax
from jax.experimental import pallas as pl
from jax.experimental.pallas import tpu as pltpu
from jax.sharding import Mesh
from jax.sharding import PartitionSpec as P

BF = jnp.bfloat16
F32 = jnp.float32
CHIPS = ("z", "y", "x")
ALL = ("z", "y", "x", "c")
HB = 8
W = 128
T = 256
HALF = 16
SPLIT = 48
ROWS = 40
MB = 1 << 20


def running(x):
    lane = lax.broadcasted_iota(jnp.int32, x.shape, 1)
    step = 1
    while step < x.shape[1]:
        x = x + jnp.where(lane >= step, pltpu.roll(x, step, axis=1), 0.0)
        step *= 2
    return x


def split3(x):
    hi = x.astype(BF).astype(F32)
    mid = (x - hi).astype(BF).astype(F32)
    return hi, mid, x - hi - mid


def dot(a, b, dims=((1,), (0,))):
    return lax.dot_general(a, b, (dims, ((), ())), preferred_element_type=F32)


def state_step(ld_ref, k_ref, v_ref):
    cum = running(ld_ref[...])
    total = cum[:, T - 1 :]
    factor = jnp.exp(total - cum)

    def state(j):
        kt = k_ref[:, j * W : (j + 1) * W].T
        decayed = (kt.astype(F32) * factor[j : j + 1, :]).astype(BF)
        return dot(decayed, v_ref[:, j * W : (j + 1) * W])

    return jnp.exp(total), state


def send_states(core_ref, ld_ref, k_ref, v_ref, out_ref):
    i = pl.program_id(0)
    decay, state = state_step(ld_ref, k_ref, v_ref)
    for j in range(HB):
        out_ref[pl.ds(pl.multiple_of(i * HB * W + j * W, W), W), :] = state(j).astype(BF)
    wide = jnp.broadcast_to(decay, (HB, W))
    first = HALF * W

    @pl.when(i == 0)
    def _():
        out_ref[first:, :] = jnp.zeros((SPLIT, W), BF)

    place = lax.broadcasted_iota(jnp.int32, (HALF, W), 0) // HB == i
    both = jnp.concatenate([wide, wide], axis=0)
    for n, term in enumerate(split3(both)):
        rows = slice(first + n * HALF, first + (n + 1) * HALF)
        old = out_ref[rows, :].astype(F32)
        out_ref[rows, :] = jnp.where(place, term, old).astype(BF)


def own_states(core_ref, ld_ref, k_ref, v_ref, out_ref, decay_ref):
    decay, state = state_step(ld_ref, k_ref, v_ref)
    for j in range(HB):
        out_ref[j] = state(j)
    decay_ref[...] = jnp.broadcast_to(decay, (HB, W))


def other_decay(recv_ref):
    first = HALF * W
    terms = [recv_ref[first + n * HALF : first + (n + 1) * HALF, :].astype(F32) for n in range(3)]
    return terms[0] + terms[1] + terms[2]


def combine(core_ref, own_ref, decay_ref, recv_ref, out_ref):
    here = decay_ref[...]
    there = other_decay(recv_ref)
    earlier = core_ref[0] == 0
    one = jnp.ones_like(here)
    a_own = jnp.where(earlier, there, one)
    a_recv = jnp.where(earlier, one, here)
    terms = split3(here * there)
    zeros = jnp.zeros((ROWS - 32 - 3, W), F32)
    for h in range(HALF):
        tail = jnp.concatenate([t[h : h + 1] for t in terms] + [zeros], axis=0)
        for r in range(4):
            own = own_ref[h, r * 32 : (r + 1) * 32, :]
            recv = recv_ref[h * W + r * 32 : h * W + (r + 1) * 32, :].astype(F32)
            body = a_own[h : h + 1] * own + a_recv[h : h + 1] * recv
            out_ref[4 * h + r] = jnp.concatenate([body, tail], axis=0).astype(BF)


def scan_chips(in_ref, out_ref):
    carry = jnp.zeros((32, W), F32)
    for j in range(in_ref.shape[0]):
        out_ref[j] = carry.astype(BF)
        x = in_ref[j].astype(F32)
        decay = x[32:33] + x[33:34] + x[34:35]
        carry = decay * carry + x[:32]


def spread_back(core_ref, chip_ref, own_ref, decay_ref, recv_ref, keep_ref, send_ref):
    earlier = core_ref[0] == 0
    decay = jnp.where(earlier, decay_ref[...], other_decay(recv_ref))
    for h in range(HALF):
        for r in range(4):
            rows = slice(r * 32, (r + 1) * 32)
            first = chip_ref[4 * h + r].astype(F32)
            own = own_ref[h, rows, :]
            recv = recv_ref[h * W + r * 32 : h * W + (r + 1) * 32, :].astype(F32)
            second = decay[h : h + 1] * first + jnp.where(earlier, own, recv)
            keep_ref[h, rows, :] = jnp.where(earlier, first, second).astype(BF)
            send_ref[h, rows, :] = jnp.where(earlier, second, first).astype(BF)


def within(ld_ref, q_ref, k_ref, v_ref, out_ref):
    cum = running(ld_ref[...])
    cols = cum.T
    n = W
    causal = lax.broadcasted_iota(jnp.int32, (n, n), 0) >= lax.broadcasted_iota(jnp.int32, (n, n), 1)
    for j in range(HB):
        at = slice(j * W, (j + 1) * W)
        row = cum[j : j + 1, :]
        col = jnp.broadcast_to(cols[:, j : j + 1], (T, n))

        def piece(t, s):
            scores = dot(q_ref[t * n : (t + 1) * n, at], k_ref[s * n : (s + 1) * n, at], ((1,), (1,)))
            gap = col[t * n : (t + 1) * n] - row[:, s * n : (s + 1) * n]
            weights = scores * jnp.exp(jnp.minimum(gap, 0.0))
            if t == s:
                weights = jnp.where(causal, weights, 0.0)
            return weights.astype(BF)

        out_ref[:n, at] = dot(piece(0, 0), v_ref[:n, at])
        lower = jnp.concatenate([piece(1, 0), piece(1, 1)], axis=1)
        out_ref[n:, at] = dot(lower, v_ref[:, at])


def finish_step(ld_ref, q_ref, inner_ref, carried_ref, gain_ref, out_ref):
    grown = jnp.exp(running(ld_ref[...])).T
    for j in range(HB):
        at = slice(j * W, (j + 1) * W)
        readout = dot(q_ref[:, at], carried_ref[j])
        numer = inner_ref[:, at] + readout * grown[:, j : j + 1]
        mean = jnp.mean(numer * numer, axis=1, keepdims=True)
        scale = lax.rsqrt(mean + 1e-6)
        out_ref[:, at] = (numer * scale * gain_ref[:, at]).astype(BF)


def finish_own(core_ref, *refs):
    finish_step(*refs)


def finish_other(core_ref, old_ref, *refs):
    finish_step(*refs)


def cost(flops, bytes_accessed):
    return pl.CostEstimate(flops=flops, bytes_accessed=bytes_accessed, transcendentals=0)


def params():
    return pltpu.CompilerParams(vmem_limit_bytes=40 * MB)


def on_device(queries, keys, values, log_decay, gain):
    core = lax.axis_index("c")
    which = core.astype(jnp.int32).reshape(1)
    heads = log_decay.shape[0]
    chips = HALF * 4

    def own(i, c):
        return c[0] * (HALF // HB) + i

    def other(i, c):
        return (1 - c[0]) * (HALF // HB) + i

    def per_half(kernel, group, ins, outs, shapes, **kw):
        return pl.pallas_call(
            kernel,
            grid_spec=pltpu.PrefetchScalarGridSpec(
                num_scalar_prefetch=1,
                grid=(HALF // HB,),
                in_specs=[s(group) for s in ins],
                out_specs=[s(group) for s in outs],
            ),
            out_shape=shapes,
            compiler_params=params(),
            **kw,
        )

    def tokens(group):
        return pl.BlockSpec((T, HB * W), lambda i, c: (0, group(i, c)))

    def decays(group):
        return pl.BlockSpec((HB, T), lambda i, c: (group(i, c), 0))

    def gains(group):
        return pl.BlockSpec((1, HB * W), lambda i, c: (0, group(i, c)))

    def states(group):
        return pl.BlockSpec((HB, W, W), lambda i, c: (i, 0, 0))

    def small(group):
        return pl.BlockSpec((HB, W), lambda i, c: (i, 0))

    def whole(group):
        return pl.BlockSpec((HALF * W + SPLIT, W), lambda i, c: (0, 0))

    swap = functools.partial(lax.ppermute, axis_name="c", perm=[(0, 1), (1, 0)])
    sent_shape = jax.ShapeDtypeStruct((HALF * W + SPLIT, W), BF)
    [sent] = per_half(
        send_states, other, [decays, tokens, tokens], [whole], [sent_shape],
        cost_estimate=cost(1 << 27, 3 * MB),
    )(which, log_decay, keys, values)
    recv = swap(sent)
    state, decay = per_half(
        own_states, own, [decays, tokens, tokens], [states, small],
        [jax.ShapeDtypeStruct((HALF, W, W), F32), jax.ShapeDtypeStruct((HALF, W), F32)],
        cost_estimate=cost(1 << 27, 3 * MB),
    )(which, log_decay, keys, values)
    smem = pl.BlockSpec(memory_space=pltpu.SMEM)
    vmem = pl.BlockSpec(memory_space=pltpu.VMEM)
    chunks = pl.pallas_call(
        combine,
        in_specs=[smem, vmem, vmem, vmem],
        out_specs=vmem,
        out_shape=jax.ShapeDtypeStruct((chips, ROWS, W), BF),
        compiler_params=params(),
    )(which, state, decay, recv)
    owned = lax.all_to_all(chunks, CHIPS, split_axis=0, concat_axis=0, tiled=True)
    before = pl.pallas_call(
        scan_chips,
        in_specs=[vmem],
        out_specs=vmem,
        out_shape=jax.ShapeDtypeStruct((chips, 32, W), BF),
        compiler_params=params(),
    )(owned)
    inner = pl.pallas_call(
        within,
        grid=(heads // HB,),
        in_specs=[pl.BlockSpec((HB, T), lambda i: (i, 0))]
        + [pl.BlockSpec((T, HB * W), lambda i: (0, i))] * 3,
        out_specs=pl.BlockSpec((T, HB * W), lambda i: (0, i)),
        out_shape=jax.ShapeDtypeStruct((T, heads * W), F32),
        compiler_params=params(),
        cost_estimate=cost(1 << 31, 10 * MB),
    )(log_decay, queries, keys, values)
    back = lax.all_to_all(before, CHIPS, split_axis=0, concat_axis=0, tiled=True)
    keep, give = pl.pallas_call(
        spread_back,
        in_specs=[smem, vmem, vmem, vmem, vmem],
        out_specs=[vmem, vmem],
        out_shape=[jax.ShapeDtypeStruct((HALF, W, W), BF)] * 2,
        compiler_params=params(),
    )(which, back, state, decay, recv)
    taken = swap(give)
    gain_row = gain.reshape(1, heads * W)
    out_shape = jax.ShapeDtypeStruct((T, heads * W), BF)
    [first] = per_half(
        finish_own, own, [decays, tokens, tokens, states, gains], [tokens], [out_shape],
        cost_estimate=cost(1 << 27, 5 * MB),
    )(which, log_decay, queries, inner, keep, gain_row)

    def left_alone(group):
        return pl.BlockSpec(memory_space=pl.ANY)

    [out] = per_half(
        finish_other, other, [left_alone, decays, tokens, tokens, states, gains], [tokens], [out_shape],
        input_output_aliases={1: 0},
        cost_estimate=cost(1 << 27, 5 * MB),
    )(which, first, log_decay, queries, inner, taken, gain_row)
    return out


def solution(mesh):
    chips = Mesh(mesh.devices.reshape(4, 4, 4, 2), ALL)
    placed = (P(ALL, None), P(ALL, None), P(ALL, None), P(None, ALL), P())
    return jax.shard_map(on_device, mesh=chips, in_specs=placed, out_specs=P(ALL, None), check_vma=False)
```

time: 172 us -> 72.7 us (0.42)
  waiting for transfers between devices: 51.3 us -> 0.01 us
  other arithmetic: 27.3 us -> 0 us
  blocking collectives: 17.2 us -> 41.1 us
  Pallas kernels: 0 us -> 22.8 us
  matrix products: 21 us -> 0 us
  local copies, waits for them, and re-layouts: 23.2 us -> 3.96 us
  between operations: 14.3 us -> 0.08 us
  starting transfers between devices: 16.5 us -> 4.55 us
    all_to_all x0 -> x2, blocking collectives: none -> 41.1 us  [the longest x1 25.3 us: on_device(): lax.all_to_all(chunks, CHIPS, split_axis=0, concat_axis=0, tiled=True)]
    all_to_all x3 -> x0, waiting for transfers between devices: 35.3 us -> none  [the longest x1 26.4 us: on_device(): lax.all_to_all(block_state[None], 'narrow', split_axis=1, concat_axis=0,...]
    pallas_call x0 -> x8, Pallas kernels: none -> 22.8 us  [the longest x1 10.3 us: on_device(): pl.pallas_call(within, grid=(heads // HB,), in_specs=[pl.BlockSpec((HB, T...]
    dot_general x13 -> x0, matrix products: 21 us -> none  [the longest x4 7.51 us: on_device(): jnp.einsum('thd,shd->hts', qpart, kpart, preferred_element_type=jnp.float32)]
    all_to_all x3 -> x0, starting transfers between devices: 16.5 us -> none  [the longest x1 5.85 us: on_device(): lax.all_to_all(prefix.astype(jnp.bfloat16), 'narrow', split_axis=0, conca...]
    all_gather x2 -> x0, waiting for transfers between devices: 15.9 us -> none  [carried_in(): pieces = jax.tree.map(lambda part: lax.all_gather(part, axis), running)]
    unnamed x34 -> x16, local copies, waits for them, and re-layouts: 16.1 us -> 3.96 us
    add x9 -> x0, other arithmetic: 10.4 us -> none  [combine(): jnp.exp(later[0])[:, None, None] * earlier[1] + later[1]]
  transfers between devices with their start and end apart: 5 -> 2, of which waited for: 4 -> 0; matrix products, arithmetic and copies ran while one was open for 18% -> 0% of each run, Pallas kernels for 0% -> 22%
where the time goes in v1:
time: 72.7 us; the launch traced here: 72.5 us
  blocking collectives  41.1 us (57%)
  Pallas kernels  22.8 us (31%)
  starting transfers between devices  4.55 us (6%)
  local copies, waits for them, and re-layouts  3.96 us (5%)
    all_to_all x1, blocking collectives, on_device(): lax.all_to_all(chunks, CHIPS, split_axis=0, concat_axis=0, tiled=True)  25.3 us
    all_to_all x1, blocking collectives, on_device(): lax.all_to_all(before, CHIPS, split_axis=0, concat_axis=0, tiled=True)  15.8 us
    pallas_call x1, Pallas kernels, on_device(): pl.pallas_call(within, grid=(heads // HB,), in_specs=[pl.BlockSpec((HB, T...  10.3 us
    pallas_call x1, Pallas kernels, on_device(): per_half(finish_own, own, [decays, tokens, tokens, states, gains], [token...  4 us
    pallas_call x1, Pallas kernels, on_device(): per_half(finish_other, other, [left_alone, decays, tokens, tokens, states...  3.97 us
    unnamed x16, local copies, waits for them, and re-layouts  3.96 us
    ppermute x1, starting transfers between devices, on_device(): taken = swap(give)  3.04 us
    pallas_call x1, Pallas kernels, on_device(): per_half(send_states, other, [decays, tokens, tokens], [whole], [sent_sha...  1.93 us
  transfers between devices with their start and end apart: 2, of which 0 were waited for; matrix products, arithmetic and copies ran while one was open for 0% of the time, Pallas kernels for 22%

profile of v1, /device:TPU:1, one launch (start us, length us, event | category | flops | bytes accessed | tf_op | source)
XLA Modules:
  0.0 72.5 jit_solution(14606550292457067122)
XLA Ops:
  0.0 0.0 copy-start
  0.0 1.6 %copy-done = bf16[256,4096]{1,0:T(8,128)(2,1)S(1)} copy-done((bf16[256,4096]{1,0:T(8,128)(2,1)S(1)}, bf16[256,4096]{1,0:T(8,128)(2,1)}, u32[]{:S(2)}) %copy-start) | copy-done | bytes 2097176
  1.6 0.0 copy-start.2
  1.6 1.6 %copy-done.2 = bf16[256,4096]{1,0:T(8,128)(2,1)S(1)} copy-done((bf16[256,4096]{1,0:T(8,128)(2,1)S(1)}, bf16[256,4096]{1,0:T(8,128)(2,1)}, u32[]{:S(2)}) %copy-start.2) | copy-done | bytes 2097176
  3.2 0.0 copy-start.5
  3.2 0.8 %copy-done.5 = f32[32,256]{1,0:T(8,128)S(1)} copy-done((f32[32,256]{1,0:T(8,128)S(1)}, f32[32,256]{1,0:T(8,128)}, u32[]{:S(2)}) %copy-start.5) | copy-done | bytes 32792
  3.9 1.9 %shard_map.57 = bf16[2096,128]{1,0:T(8,128)(2,1)S(1)} custom-call(s32[1]{0:T(128)} %bitcast.core_ref, f32[32,256]{1,0:T(8,128)S(1)} %copy-done.5, bf16[256,4096]{1,0:T(8,128)(2,1)S(1)} %copy-done, bf16[256,4096]{1,0:T(8,128)(2,1)S(1)} %copy-done.2), custom_call_target="tpu_custom_call" | custom-call | flops 134217728 | bytes 3145728 | tf_op jit(solution)/shard_map/pallas_call | solution.py:226
  5.9 1.5 %collective-permute-start = (bf16[2096,128]{1,0:T(8,128)(2,1)S(1)}, bf16[2096,128]{1,0:T(8,128)(2,1)S(1)}, u32[]{:S(2)}, u32[]{:S(2)}) collective-permute-start(bf16[2096,128]{1,0:T(8,128)(2,1)S(1)} %shard_map.57), channel_id=1, source_target_pairs={{0,1},{1,0},{2,3},{3,2},{4,5},{5,4},{6,7},{7,6},{8,9},{9,8},{10,11... | collective-permute-start | bytes 1609736 | tf_op jit(solution)/shard_map/ppermute | solution.py:230
  7.4 1.9 %shard_map.56 = (f32[16,128,128]{2,1,0:T(8,128)S(1)}, f32[16,128]{1,0:T(8,128)S(1)}) custom-call(s32[1]{0:T(128)} %bitcast.core_ref, f32[32,256]{1,0:T(8,128)S(1)} %copy-done.5, bf16[256,4096]{1,0:T(8,128)(2,1)S(1)} %copy-done, bf16[256,4096]{1,0:T(8,128)(2,1)S(1)} %copy-done.2), custom_call_target="tpu_custom_call" | custom-call | flops 134217728 | bytes 3145728 | tf_op jit(solution)/shard_map/pallas_call | solution.py:231
  9.3 0.0 collective-permute-done.recv_ref
  9.3 0.0 copy-start.4
  9.3 0.2 shard_map.58
  9.5 25.3 %all_to_all.10.in_ref = bf16[64,40,128]{2,1,0:T(8,128)(2,1)S(1)} all-to-all(bf16[64,40,128]{2,1,0:T(8,128)(2,1)S(1)} %shard_map.58), channel_id=1, replica_groups=mesh['z'=4,'y'=4,'x'=4,'c'=2] {'z','y','x'}, dimensions={0} | all-to-all | bytes 1310720 | tf_op jit(solution)/shard_map/all_to_all | solution.py:245
  34.8 0.0 copy-start.1
  34.8 0.0 copy-start.3
  34.8 0.0 copy-start.6
  34.8 0.2 shard_map.59
  35.0 15.8 %all_to_all.11.chip_ref = bf16[64,32,128]{2,1,0:T(8,128)(2,1)S(1)} all-to-all(bf16[64,32,128]{2,1,0:T(8,128)(2,1)S(1)} %shard_map.59), channel_id=1, replica_groups=mesh['z'=4,'y'=4,'x'=4,'c'=2] {'z','y','x'}, dimensions={0} | all-to-all | bytes 1048576 | tf_op jit(solution)/shard_map/all_to_all | solution.py:263
  50.8 0.3 shard_map.60
  51.1 0.0 copy-start.7
  51.1 3.0 %collective-permute-start.1 = (bf16[16,128,128]{2,1,0:T(8,128)(2,1)S(1)}, bf16[16,128,128]{2,1,0:T(8,128)(2,1)S(1)}, u32[]{:S(2)}, u32[]{:S(2)}) collective-permute-start(bf16[16,128,128]{2,1,0:T(8,128)(2,1)S(1)} %get-tuple-element.12), channel_id=1, source_target_pairs={{0,1},{1,0},{2,3},{3,2},{4,5},{5,4},{6,7},{7,6},{8,9},{9,8},{10,11... | collective-permute-start | bytes 1572872 | tf_op jit(solution)/shard_map/ppermute | solution.py:271
  54.1 0.0 copy-done.4
  54.1 0.0 copy-done.1
  54.1 0.0 copy-done.3
  54.1 0.0 copy-done.6
  54.1 10.3 %shard_map.55.refs_2_ = f32[256,4096]{1,0:T(8,128)S(1)} custom-call(f32[32,256]{1,0:T(8,128)S(1)} %copy-done.6, bf16[256,4096]{1,0:T(8,128)(2,1)S(1)} %copy-done.4, bf16[256,4096]{1,0:T(8,128)(2,1)S(1)} %copy-done.1, bf16[256,4096]{1,0:T(8,128)(2,1)S(1)} %copy-done.3), custom_call_target="tpu_custom_call" | custom-call | flops 2147483648 | bytes 10485760 | tf_op jit(solution)/shard_map/pallas_call | solution.py:253
  64.5 0.0 copy-done.7
  64.5 4.0 %shard_map.61.old_ref = bf16[256,4096]{1,0:T(8,128)(2,1)} custom-call(s32[1]{0:T(128)} %bitcast.core_ref, f32[32,256]{1,0:T(8,128)S(1)} %copy-done.6, bf16[256,4096]{1,0:T(8,128)(2,1)S(1)} %copy-done.4, f32[256,4096]{1,0:T(8,128)S(1)} %shard_map.55.refs_2_, bf16[16,128,128]{2,1,0:T(8,128)(2,1)S(1)} %get-tuple-element.11.refs_3_, f32[1,4096]{1,0:T(1,128)S(1)} %bitcast.2), custom_call_target="tpu_custom_call" | custom-call | flops 134217728 | bytes 5242880 | tf_op jit(solution)/shard_map/pallas_call | solution.py:274
  68.5 0.0 collective-permute-done.1.refs_3_
  68.5 4.0 %shard_map.62 = bf16[256,4096]{1,0:T(8,128)(2,1)} custom-call(s32[1]{0:T(128)} %bitcast.core_ref, bf16[256,4096]{1,0:T(8,128)(2,1)} %shard_map.61.old_ref, f32[32,256]{1,0:T(8,128)S(1)} %copy-done.6, bf16[256,4096]{1,0:T(8,128)(2,1)S(1)} %copy-done.4, f32[256,4096]{1,0:T(8,128)S(1)} %shard_map.55.refs_2_, ...), custom_call_target="tpu_custom_call", output_to_operand_aliasing={{}: (1, {})} | custom-call | flops 134217728 | bytes 5242880 | tf_op jit(solution)/shard_map/pallas_call | solution.py:282
Async XLA Ops:
  0.0 1.6 %copy-start = (bf16[256,4096]{1,0:T(8,128)(2,1)S(1)}, bf16[256,4096]{1,0:T(8,128)(2,1)}, u32[]{:S(2)}) copy-start(bf16[256,4096]{1,0:T(8,128)(2,1)} %k_ref.5) | copy-start | bytes 6291460
  1.6 1.6 %copy-start.2 = (bf16[256,4096]{1,0:T(8,128)(2,1)S(1)}, bf16[256,4096]{1,0:T(8,128)(2,1)}, u32[]{:S(2)}) copy-start(bf16[256,4096]{1,0:T(8,128)(2,1)} %v_ref.5) | copy-start | bytes 6291460
  3.2 0.8 %copy-start.5 = (f32[32,256]{1,0:T(8,128)S(1)}, f32[32,256]{1,0:T(8,128)}, u32[]{:S(2)}) copy-start(f32[32,256]{1,0:T(8,128)} %refs_0_.3) | copy-start | bytes 98308
  5.9 3.4 %collective-permute-start = (bf16[2096,128]{1,0:T(8,128)(2,1)S(1)}, bf16[2096,128]{1,0:T(8,128)(2,1)S(1)}, u32[]{:S(2)}, u32[]{:S(2)}) collective-permute-start(bf16[2096,128]{1,0:T(8,128)(2,1)S(1)} %shard_map.57), channel_id=1, source_target_pairs={{0,1},{1,0},{2,3},{3,2},{4,5},{5,4},{6,7},{7,6},{8,9},{9,8},{10,11... | collective-permute-start | bytes 1609736 | tf_op jit(solution)/shard_map/ppermute | solution.py:230
  9.3 44.8 %copy-start.4 = (bf16[256,4096]{1,0:T(8,128)(2,1)S(1)}, bf16[256,4096]{1,0:T(8,128)(2,1)}, u32[]{:S(2)}) copy-start(bf16[256,4096]{1,0:T(8,128)(2,1)} %refs_1_.3) | copy-start | bytes 6291460
  34.8 19.3 %copy-start.1 = (bf16[256,4096]{1,0:T(8,128)(2,1)S(1)}, bf16[256,4096]{1,0:T(8,128)(2,1)}, u32[]{:S(2)}) copy-start(bf16[256,4096]{1,0:T(8,128)(2,1)} %k_ref.5) | copy-start | bytes 6291460
  34.8 19.3 %copy-start.3 = (bf16[256,4096]{1,0:T(8,128)(2,1)S(1)}, bf16[256,4096]{1,0:T(8,128)(2,1)}, u32[]{:S(2)}) copy-start(bf16[256,4096]{1,0:T(8,128)(2,1)} %v_ref.5) | copy-start | bytes 6291460
  34.8 19.3 %copy-start.6 = (f32[32,256]{1,0:T(8,128)S(1)}, f32[32,256]{1,0:T(8,128)}, u32[]{:S(2)}) copy-start(f32[32,256]{1,0:T(8,128)} %refs_0_.3) | copy-start | bytes 98308
  51.1 13.4 %copy-start.7 = (f32[4096]{0:T(1024)S(1)}, f32[4096]{0:T(1024)}, u32[]{:S(2)}) copy-start(f32[4096]{0:T(1024)} %param.9) | copy-start | bytes 49156
  51.1 17.4 %collective-permute-start.1 = (bf16[16,128,128]{2,1,0:T(8,128)(2,1)S(1)}, bf16[16,128,128]{2,1,0:T(8,128)(2,1)S(1)}, u32[]{:S(2)}, u32[]{:S(2)}) collective-permute-start(bf16[16,128,128]{2,1,0:T(8,128)(2,1)S(1)} %get-tuple-element.12), channel_id=1, source_target_pairs={{0,1},{1,0},{2,3},{3,2},{4,5},{5,4},{6,7},{7,6},{8,9},{9,8},{10,11... | collective-permute-start | bytes 1572872 | tf_op jit(solution)/shard_map/ppermute | solution.py:271

commit v2 on v1

--- a/solution.py
+++ b/solution.py
@@ -174,11 +174,12 @@
 
 
 def params():
-    return pltpu.CompilerParams(vmem_limit_bytes=40 * MB)
+    return pltpu.CompilerParams(vmem_limit_bytes=12 * MB)
 
 
 def on_device(queries, keys, values, log_decay, gain):
     core = lax.axis_index("c")
+    keys, values = (pltpu.with_memory_space_constraint(a, pltpu.HBM) for a in (keys, values))
     which = core.astype(jnp.int32).reshape(1)
     heads = log_decay.shape[0]
     chips = HALF * 4
@@ -242,24 +243,26 @@
         out_shape=jax.ShapeDtypeStruct((chips, ROWS, W), BF),
         compiler_params=params(),
     )(which, state, decay, recv)
+    chunks, queries = lax.optimization_barrier((chunks, queries))
     owned = lax.all_to_all(chunks, CHIPS, split_axis=0, concat_axis=0, tiled=True)
-    before = pl.pallas_call(
-        scan_chips,
-        in_specs=[vmem],
-        out_specs=vmem,
-        out_shape=jax.ShapeDtypeStruct((chips, 32, W), BF),
-        compiler_params=params(),
-    )(owned)
     inner = pl.pallas_call(
         within,
         grid=(heads // HB,),
         in_specs=[pl.BlockSpec((HB, T), lambda i: (i, 0))]
         + [pl.BlockSpec((T, HB * W), lambda i: (0, i))] * 3,
         out_specs=pl.BlockSpec((T, HB * W), lambda i: (0, i)),
-        out_shape=jax.ShapeDtypeStruct((T, heads * W), F32),
+        out_shape=pltpu.HBM((T, heads * W), F32),
         compiler_params=params(),
         cost_estimate=cost(1 << 31, 10 * MB),
     )(log_decay, queries, keys, values)
+    owned, inner = lax.optimization_barrier((owned, inner))
+    before = pl.pallas_call(
+        scan_chips,
+        in_specs=[vmem],
+        out_specs=vmem,
+        out_shape=jax.ShapeDtypeStruct((chips, 32, W), BF),
+        compiler_params=params(),
+    )(owned)
     back = lax.all_to_all(before, CHIPS, split_axis=0, concat_axis=0, tiled=True)
     keep, give = pl.pallas_call(
         spread_back,

time: 72.7 us -> 68.9 us (0.948)
  blocking collectives: 41.1 us -> 20 us
  starting transfers between devices: 4.55 us -> 15.1 us
  Pallas kernels: 22.8 us -> 27.9 us
  waiting for transfers between devices: 0.01 us -> 1.84 us
    all_to_all x1 -> x0, blocking collectives: 25.3 us -> none  [on_device(): lax.all_to_all(chunks, CHIPS, split_axis=0, concat_axis=0, tiled=True)]
    all_to_all x0 -> x1, starting transfers between devices: none -> 11.4 us  [on_device(): lax.all_to_all(chunks, CHIPS, split_axis=0, concat_axis=0, tiled=True)]
    all_to_all x1, blocking collectives: 15.8 us -> 20 us  [on_device(): lax.all_to_all(before, CHIPS, split_axis=0, concat_axis=0, tiled=True)]
    all_to_all x0 -> x1, waiting for transfers between devices: none -> 1.83 us  [on_device(): lax.all_to_all(chunks, CHIPS, split_axis=0, concat_axis=0, tiled=True)]
    pallas_call x1, Pallas kernels: 10.3 us -> 12.2 us  [on_device(): pl.pallas_call(within, grid=(heads // HB,), in_specs=[pl.BlockSpec((HB, T...]
    pallas_call x1, Pallas kernels: 0.17 us -> 1.41 us  [on_device(): pl.pallas_call(scan_chips, in_specs=[vmem], out_specs=vmem, out_shape=jax...]
    pallas_call x1, Pallas kernels: 1.93 us -> 2.99 us  [on_device(): per_half(send_states, other, [decays, tokens, tokens], [whole], [sent_sha...]
    pallas_call x1, Pallas kernels: 1.9 us -> 2.95 us  [on_device(): per_half(own_states, own, [decays, tokens, tokens], [states, small], [jax...]
  transfers between devices with their start and end apart: 2 -> 3, of which waited for: 0 -> 1; matrix products, arithmetic and copies ran while one was open for 0% -> 0% of each run, Pallas kernels for 22% -> 28%
where the time goes in v2:
time: 68.9 us; the launch traced here: 68.5 us
  Pallas kernels  27.9 us (40%)
  blocking collectives  20 us (29%)
  starting transfers between devices  15.1 us (22%)
  local copies, waits for them, and re-layouts  3.45 us (5%)
  waiting for transfers between devices  1.84 us (3%)
    all_to_all x1, blocking collectives, on_device(): lax.all_to_all(before, CHIPS, split_axis=0, concat_axis=0, tiled=True)  20 us
    pallas_call x1, Pallas kernels, on_device(): pl.pallas_call(within, grid=(heads // HB,), in_specs=[pl.BlockSpec((HB, T...  12.2 us
    all_to_all x1, starting transfers between devices, on_device(): lax.all_to_all(chunks, CHIPS, split_axis=0, concat_axis=0, tiled=True)  11.4 us
    pallas_call x1, Pallas kernels, on_device(): per_half(finish_other, other, [left_alone, decays, tokens, tokens, states...  3.97 us
    pallas_call x1, Pallas kernels, on_device(): per_half(finish_own, own, [decays, tokens, tokens, states, gains], [token...  3.97 us
    unnamed x16, local copies, waits for them, and re-layouts  3.45 us
    pallas_call x1, Pallas kernels, on_device(): per_half(send_states, other, [decays, tokens, tokens], [whole], [sent_sha...  2.99 us
    pallas_call x1, Pallas kernels, on_device(): per_half(own_states, own, [decays, tokens, tokens], [states, small], [jax...  2.95 us
  transfers between devices with their start and end apart: 3, of which 1 were waited for; matrix products, arithmetic and copies ran while one was open for 0% of the time, Pallas kernels for 28%

profile of v2, /device:TPU:1, one launch (start us, length us, event | category | flops | bytes accessed | tf_op | source)
XLA Modules:
  0.0 68.5 jit_solution(16238126724183717656)
XLA Ops:
  0.0 0.0 copy-start.5
  0.0 0.8 %copy-done.5 = f32[32,256]{1,0:T(8,128)S(1)} copy-done((f32[32,256]{1,0:T(8,128)S(1)}, f32[32,256]{1,0:T(8,128)}, u32[]{:S(2)}) %copy-start.5) | copy-done | bytes 32792
  0.8 3.0 %shard_map.56 = bf16[2096,128]{1,0:T(8,128)(2,1)S(1)} custom-call(s32[1]{0:T(128)} %bitcast.core_ref, f32[32,256]{1,0:T(8,128)S(1)} %copy-done.5, bf16[256,4096]{1,0:T(8,128)(2,1)} %k_ref.5, bf16[256,4096]{1,0:T(8,128)(2,1)} %v_ref.5), custom_call_target="tpu_custom_call" | custom-call | flops 134217728 | bytes 3145728 | tf_op jit(solution)/shard_map/pallas_call | solution.py:227
  3.8 1.5 %collective-permute-start = (bf16[2096,128]{1,0:T(8,128)(2,1)S(1)}, bf16[2096,128]{1,0:T(8,128)(2,1)S(1)}, u32[]{:S(2)}, u32[]{:S(2)}) collective-permute-start(bf16[2096,128]{1,0:T(8,128)(2,1)S(1)} %shard_map.56), channel_id=1, source_target_pairs={{0,1},{1,0},{2,3},{3,2},{4,5},{5,4},{6,7},{7,6},{8,9},{9,8},{10,11... | collective-permute-start | bytes 1609736 | tf_op jit(solution)/shard_map/ppermute | solution.py:231
  5.3 3.0 %shard_map.55 = (f32[16,128,128]{2,1,0:T(8,128)S(1)}, f32[16,128]{1,0:T(8,128)S(1)}) custom-call(s32[1]{0:T(128)} %bitcast.core_ref, f32[32,256]{1,0:T(8,128)S(1)} %copy-done.5, bf16[256,4096]{1,0:T(8,128)(2,1)} %k_ref.5, bf16[256,4096]{1,0:T(8,128)(2,1)} %v_ref.5), custom_call_target="tpu_custom_call" | custom-call | flops 134217728 | bytes 3145728 | tf_op jit(solution)/shard_map/pallas_call | solution.py:232
  8.2 0.0 copy-start.1
  8.2 0.0 copy-start.6
  8.2 0.0 collective-permute-done.recv_ref
  8.3 0.2 shard_map.57
  8.5 0.0 copy-start.2
  8.5 0.8 %copy-done.2 = bf16[64,40,128]{2,1,0:T(8,128)(2,1)} copy-done((bf16[64,40,128]{2,1,0:T(8,128)(2,1)}, bf16[64,40,128]{2,1,0:T(8,128)(2,1)S(1)}, u32[]{:S(2)}) %copy-start.2) | copy-done | bytes 655384
  9.3 0.0 copy-start.3
  9.3 0.8 %copy-done.3 = bf16[2096,128]{1,0:T(8,128)(2,1)} copy-done((bf16[2096,128]{1,0:T(8,128)(2,1)}, bf16[2096,128]{1,0:T(8,128)(2,1)S(1)}, u32[]{:S(2)}) %copy-start.3) | copy-done | bytes 536600
  10.1 11.4 %all-to-all-start = ((bf16[64,40,128]{2,1,0:T(8,128)(2,1)}), bf16[64,40,128]{2,1,0:T(8,128)(2,1)}, u32[]{:S(2)}, u32[]{:S(2)}) async-start(bf16[64,40,128]{2,1,0:T(8,128)(2,1)} %copy-done.2), calls=%async_computation | async-start | bytes 1310720 | tf_op jit(solution)/shard_map/all_to_all | solution.py:247
  21.5 0.0 copy-done.1
  21.5 0.0 copy-done.6
  21.6 0.0 copy-start.7
  21.6 12.2 %shard_map.58.refs_2_ = f32[256,4096]{1,0:T(8,128)} custom-call(f32[32,256]{1,0:T(8,128)S(1)} %copy-done.6, bf16[256,4096]{1,0:T(8,128)(2,1)S(1)} %copy-done.1, bf16[256,4096]{1,0:T(8,128)(2,1)} %k_ref.5, bf16[256,4096]{1,0:T(8,128)(2,1)} %v_ref.5), custom_call_target="tpu_custom_call" | custom-call | flops 2147483648 | bytes 10485760 | tf_op jit(solution)/shard_map/pallas_call | solution.py:248
  33.7 1.8 %all-to-all-done.in_ref = bf16[64,40,128]{2,1,0:T(8,128)(2,1)} async-done(((bf16[64,40,128]{2,1,0:T(8,128)(2,1)}), bf16[64,40,128]{2,1,0:T(8,128)(2,1)}, u32[]{:S(2)}, u32[]{:S(2)}) %all-to-all-start) | async-done | bytes 655392 | tf_op jit(solution)/shard_map/all_to_all | solution.py:247
  35.6 0.0 copy-start
  35.6 1.4 %shard_map.59 = bf16[64,32,128]{2,1,0:T(8,128)(2,1)S(1)} custom-call(bf16[64,40,128]{2,1,0:T(8,128)(2,1)} %all-to-all-done.in_ref), custom_call_target="tpu_custom_call" | custom-call | tf_op jit(solution)/shard_map/pallas_call | solution.py:259
  37.0 20.0 %all_to_all.10.chip_ref = bf16[64,32,128]{2,1,0:T(8,128)(2,1)S(1)} all-to-all(bf16[64,32,128]{2,1,0:T(8,128)(2,1)S(1)} %shard_map.59), channel_id=1, replica_groups=mesh['z'=4,'y'=4,'x'=4,'c'=2] {'z','y','x'}, dimensions={0} | all-to-all | bytes 1048576 | tf_op jit(solution)/shard_map/all_to_all | solution.py:266
  57.0 0.0 copy-start.4
  57.0 1.0 %copy-done.4 = bf16[2096,128]{1,0:T(8,128)(2,1)S(1)} copy-done((bf16[2096,128]{1,0:T(8,128)(2,1)S(1)}, bf16[2096,128]{1,0:T(8,128)(2,1)}, u32[]{:S(2)}) %copy-start.4) | copy-done | bytes 536600
  58.1 0.3 shard_map.60
  58.4 2.2 %collective-permute-start.1 = (bf16[16,128,128]{2,1,0:T(8,128)(2,1)S(1)}, bf16[16,128,128]{2,1,0:T(8,128)(2,1)S(1)}, u32[]{:S(2)}, u32[]{:S(2)}) collective-permute-start(bf16[16,128,128]{2,1,0:T(8,128)(2,1)S(1)} %get-tuple-element.20), channel_id=1, source_target_pairs={{0,1},{1,0},{2,3},{3,2},{4,5},{5,4},{6,7},{7,6},{8,9},{9,8},{10,11... | collective-permute-start | bytes 1572872 | tf_op jit(solution)/shard_map/ppermute | solution.py:274
  60.5 0.0 copy-done.7
  60.5 0.0 copy-done
  60.5 4.0 %shard_map.61.old_ref = bf16[256,4096]{1,0:T(8,128)(2,1)} custom-call(s32[1]{0:T(128)} %bitcast.core_ref, f32[32,256]{1,0:T(8,128)S(1)} %copy-done.6, bf16[256,4096]{1,0:T(8,128)(2,1)S(1)} %copy-done.1, f32[256,4096]{1,0:T(8,128)S(1)} %copy-done, bf16[16,128,128]{2,1,0:T(8,128)(2,1)S(1)} %get-tuple-element.19.refs_3_, f32[1,4096]{1,0:T(1,128)S(1)} %bitcast.2), custom_call_target="tpu_custom_call" | custom-call | flops 134217728 | bytes 5242880 | tf_op jit(solution)/shard_map/pallas_call | solution.py:277
  64.5 0.0 collective-permute-done.1.refs_3_
  64.5 4.0 %shard_map.62 = bf16[256,4096]{1,0:T(8,128)(2,1)} custom-call(s32[1]{0:T(128)} %bitcast.core_ref, bf16[256,4096]{1,0:T(8,128)(2,1)} %shard_map.61.old_ref, f32[32,256]{1,0:T(8,128)S(1)} %copy-done.6, bf16[256,4096]{1,0:T(8,128)(2,1)S(1)} %copy-done.1, f32[256,4096]{1,0:T(8,128)S(1)} %copy-done, ...), custom_call_target="tpu_custom_call", output_to_operand_aliasing={{}: (1, {})} | custom-call | flops 134217728 | bytes 5242880 | tf_op jit(solution)/shard_map/pallas_call | solution.py:285
Async XLA Ops:
  0.0 0.8 %copy-start.5 = (f32[32,256]{1,0:T(8,128)S(1)}, f32[32,256]{1,0:T(8,128)}, u32[]{:S(2)}) copy-start(f32[32,256]{1,0:T(8,128)} %refs_0_.3) | copy-start | bytes 98308
  3.8 4.5 %collective-permute-start = (bf16[2096,128]{1,0:T(8,128)(2,1)S(1)}, bf16[2096,128]{1,0:T(8,128)(2,1)S(1)}, u32[]{:S(2)}, u32[]{:S(2)}) collective-permute-start(bf16[2096,128]{1,0:T(8,128)(2,1)S(1)} %shard_map.56), channel_id=1, source_target_pairs={{0,1},{1,0},{2,3},{3,2},{4,5},{5,4},{6,7},{7,6},{8,9},{9,8},{10,11... | collective-permute-start | bytes 1609736 | tf_op jit(solution)/shard_map/ppermute | solution.py:231
  8.2 13.3 %copy-start.1 = (bf16[256,4096]{1,0:T(8,128)(2,1)S(1)}, bf16[256,4096]{1,0:T(8,128)(2,1)}, u32[]{:S(2)}) copy-start(bf16[256,4096]{1,0:T(8,128)(2,1)} %refs_1_.1) | copy-start | bytes 6291460
  8.2 13.3 %copy-start.6 = (f32[32,256]{1,0:T(8,128)S(1)}, f32[32,256]{1,0:T(8,128)}, u32[]{:S(2)}) copy-start(f32[32,256]{1,0:T(8,128)} %refs_0_.3) | copy-start | bytes 98308
  8.5 0.8 %copy-start.2 = (bf16[64,40,128]{2,1,0:T(8,128)(2,1)}, bf16[64,40,128]{2,1,0:T(8,128)(2,1)S(1)}, u32[]{:S(2)}) copy-start(bf16[64,40,128]{2,1,0:T(8,128)(2,1)S(1)} %shard_map.57) | copy-start | bytes 1966084
  9.3 0.8 %copy-start.3 = (bf16[2096,128]{1,0:T(8,128)(2,1)}, bf16[2096,128]{1,0:T(8,128)(2,1)S(1)}, u32[]{:S(2)}) copy-start(bf16[2096,128]{1,0:T(8,128)(2,1)S(1)} %collective-permute-done.recv_ref) | copy-start | bytes 1609732
  10.1 25.5 %all-to-all-start = ((bf16[64,40,128]{2,1,0:T(8,128)(2,1)}), bf16[64,40,128]{2,1,0:T(8,128)(2,1)}, u32[]{:S(2)}, u32[]{:S(2)}) async-start(bf16[64,40,128]{2,1,0:T(8,128)(2,1)} %copy-done.2), calls=%async_computation | async-start | bytes 1310720 | tf_op jit(solution)/shard_map/all_to_all | solution.py:247
  21.6 39.0 %copy-start.7 = (f32[4096]{0:T(1024)S(1)}, f32[4096]{0:T(1024)}, u32[]{:S(2)}) copy-start(f32[4096]{0:T(1024)} %param.9) | copy-start | bytes 49156
  35.6 25.0 %copy-start = (f32[256,4096]{1,0:T(8,128)S(1)}, f32[256,4096]{1,0:T(8,128)}, u32[]{:S(2)}) copy-start(f32[256,4096]{1,0:T(8,128)} %shard_map.58.refs_2_) | copy-start | bytes 12582916
  57.0 1.0 %copy-start.4 = (bf16[2096,128]{1,0:T(8,128)(2,1)S(1)}, bf16[2096,128]{1,0:T(8,128)(2,1)}, u32[]{:S(2)}) copy-start(bf16[2096,128]{1,0:T(8,128)(2,1)} %copy-done.3) | copy-start | bytes 1609732
  58.4 6.2 %collective-permute-start.1 = (bf16[16,128,128]{2,1,0:T(8,128)(2,1)S(1)}, bf16[16,128,128]{2,1,0:T(8,128)(2,1)S(1)}, u32[]{:S(2)}, u32[]{:S(2)}) collective-permute-start(bf16[16,128,128]{2,1,0:T(8,128)(2,1)S(1)} %get-tuple-element.20), channel_id=1, source_target_pairs={{0,1},{1,0},{2,3},{3,2},{4,5},{5,4},{6,7},{7,6},{8,9},{9,8},{10,11... | collective-permute-start | bytes 1572872 | tf_op jit(solution)/shard_map/ppermute | solution.py:274

commit v3 on v1

v3 whole, which is shorter than its diff:
```python
import functools

import jax
import jax.numpy as jnp
from jax import lax
from jax.experimental import pallas as pl
from jax.experimental.pallas import tpu as pltpu
from jax.sharding import Mesh
from jax.sharding import PartitionSpec as P

BF = jnp.bfloat16
F32 = jnp.float32
CHIPS = ("z", "y", "x")
ALL = ("z", "y", "x", "c")
HB = 8
W = 128
T = 256
HALF = 16
SPLIT = 48
ROWS = 40
PART = 4
MB = 1 << 20
LIMIT = 12
FINISH = 20


def running(x):
    lane = lax.broadcasted_iota(jnp.int32, x.shape, 1)
    step = 1
    while step < x.shape[1]:
        x = x + jnp.where(lane >= step, pltpu.roll(x, step, axis=1), 0.0)
        step *= 2
    return x


def split3(x):
    hi = x.astype(BF).astype(F32)
    mid = (x - hi).astype(BF).astype(F32)
    return hi, mid, x - hi - mid


def dot(a, b, dims=((1,), (0,))):
    return lax.dot_general(a, b, (dims, ((), ())), preferred_element_type=F32)


def load(core_ref, refs, bufs, sem, own):
    half = core_ref[0] if own else 1 - core_ref[0]
    columns = pl.ds(pl.multiple_of(half * HALF * W, HALF * W), HALF * W)
    rows = pl.ds(pl.multiple_of(half * HALF, HALF), HALF)
    views = [r.at[:, columns] for r in refs[:-1]] + [refs[-1].at[rows, :]]
    copies = [pltpu.make_async_copy(v, b, sem.at[n]) for n, (v, b) in enumerate(zip(views, bufs))]
    for c in reversed(copies):
        c.start()
    return copies


def states_of(core_ref, k_ref, v_ref, ld_ref, kbuf, vbuf, dbuf, sem, own, put):
    k_in, v_in, d_in = load(core_ref, (k_ref, v_ref, ld_ref), (kbuf, vbuf, dbuf), sem, own)
    d_in.wait()
    cum = running(dbuf[...])
    total = cum[:, T - 1 :]
    factor = jnp.exp(total - cum)
    k_in.wait()

    def decayed(j):
        kt = kbuf[:, j * W : (j + 1) * W].T
        return (kt.astype(F32) * factor[j : j + 1, :]).astype(BF)

    ready = [decayed(0), decayed(1)]
    v_in.wait()
    for j in range(HALF):
        if j + 2 < HALF:
            ready.append(decayed(j + 2))
        put(j, dot(ready[j], vbuf[:, j * W : (j + 1) * W]))
    return jnp.broadcast_to(jnp.exp(total), (HALF, W))


def send_states(core_ref, k_ref, v_ref, ld_ref, out_ref, *scratch):
    def put(j, state):
        out_ref[j * W : (j + 1) * W, :] = state.astype(BF)

    decay = states_of(core_ref, k_ref, v_ref, ld_ref, *scratch, own=False, put=put)
    first = HALF * W
    for n, term in enumerate(split3(decay)):
        out_ref[first + n * HALF : first + (n + 1) * HALF, :] = term.astype(BF)


def own_states(core_ref, k_ref, v_ref, ld_ref, out_ref, decay_ref, *scratch):
    def put(j, state):
        out_ref[j] = state

    decay_ref[...] = states_of(core_ref, k_ref, v_ref, ld_ref, *scratch, own=True, put=put)


def other_decay(recv_ref):
    first = HALF * W
    terms = [recv_ref[first + n * HALF : first + (n + 1) * HALF, :].astype(F32) for n in range(3)]
    return terms[0] + terms[1] + terms[2]


def combine(core_ref, own_ref, decay_ref, recv_ref, out_ref, first_ref, first_decay_ref):
    here = decay_ref[...]
    there = other_decay(recv_ref)
    earlier = core_ref[0] == 0
    one = jnp.ones_like(here)
    a_own = jnp.where(earlier, there, one)
    a_recv = jnp.where(earlier, one, here)
    first_decay_ref[...] = jnp.where(earlier, here, there)
    terms = split3(here * there)
    zeros = jnp.zeros((ROWS - 32 - 3, W), F32)
    for h in range(HALF):
        tail = jnp.concatenate([t[h : h + 1] for t in terms] + [zeros], axis=0)
        for r in range(4):
            rows = slice(r * 32, (r + 1) * 32)
            own = own_ref[h, rows, :]
            recv = recv_ref[h * W + r * 32 : h * W + (r + 1) * 32, :].astype(F32)
            body = a_own[h : h + 1] * own + a_recv[h : h + 1] * recv
            out_ref[4 * h + r] = jnp.concatenate([body, tail], axis=0).astype(BF)
            first_ref[h, rows, :] = jnp.where(earlier, own, recv).astype(BF)


def scan_chips(in_ref, out_ref):
    carry = jnp.zeros((32, W), F32)
    for j in range(in_ref.shape[0]):
        out_ref[j] = carry.astype(BF)
        x = in_ref[j].astype(F32)
        decay = x[32:33] + x[33:34] + x[34:35]
        carry = decay * carry + x[:32]


def spread_back(core_ref, chip_ref, first_ref, first_decay_ref, keep_ref, send_ref):
    earlier = core_ref[0] == 0
    decay = first_decay_ref[...]
    for h in range(HALF):
        for r in range(4):
            rows = slice(r * 32, (r + 1) * 32)
            first = chip_ref[4 * h + r].astype(F32)
            second = decay[h : h + 1] * first + first_ref[h, rows, :].astype(F32)
            keep_ref[h, rows, :] = jnp.where(earlier, first, second).astype(BF)
            send_ref[h, rows, :] = jnp.where(earlier, second, first).astype(BF)


def within(ld_ref, q_ref, k_ref, v_ref, out_ref):
    cum = running(ld_ref[...])
    cols = cum.T
    n = W
    causal = lax.broadcasted_iota(jnp.int32, (n, n), 0) >= lax.broadcasted_iota(jnp.int32, (n, n), 1)

    def scores(j):
        at = slice(j * W, (j + 1) * W)
        nt = ((1,), (1,))
        return dot(q_ref[:n, at], k_ref[:n, at], nt), dot(q_ref[n:, at], k_ref[:, at], nt)

    def weights(j, upper, lower):
        row, col = cum[j : j + 1, :], cols[:, j : j + 1]

        def decay(t, s):
            gap = col[t * n : (t + 1) * n] - row[:, s * n : (s + 1) * n]
            if t == s:
                gap = jnp.where(causal, gap, -1e30)
            return jnp.exp(jnp.minimum(gap, 0.0))

        low = [lower[:, :n] * decay(1, 0), lower[:, n:] * decay(1, 1)]
        return (upper * decay(0, 0)).astype(BF), jnp.concatenate(low, axis=1).astype(BF)

    def total(j, upper, lower):
        at = slice(j * W, (j + 1) * W)
        out_ref[:n, at] = dot(upper, v_ref[:n, at])
        out_ref[n:, at] = dot(lower, v_ref[:, at])

    following = scores(0)
    waiting = None
    for j in range(HB):
        current = following
        if j + 1 < HB:
            following = scores(j + 1)
        made = weights(j, *current)
        if waiting is not None:
            total(j - 1, *waiting)
        waiting = made
    total(HB - 1, *waiting)


def within_half(core_ref, *refs):
    within(*refs)


def finish_half(core_ref, ld_ref, q_ref, inner_ref, carried_ref, gain_ref, out_ref, buf, sem, own, arrive):
    half = core_ref[0] if own else 1 - core_ref[0]
    grown = jnp.exp(running(ld_ref[pl.ds(pl.multiple_of(half * HALF, HALF), HALF), :])).T
    ones = jnp.full((W, W), 1.0 / W, BF)

    def columns(j, count=1):
        return pl.ds(pl.multiple_of(half * HALF * W + j * W, W), count * W)

    def readout(j):
        return dot(q_ref[:, columns(j)], carried_ref[j])

    copies = []
    following = readout(0)
    for j in range(HALF):
        current = following
        if j + 1 < HALF:
            following = readout(j + 1)
        arrive(j)
        numer = inner_ref[:, j * W : (j + 1) * W] + current * grown[:, j : j + 1]
        mean = dot((numer * numer).astype(BF), ones)
        buf[:, j * W : (j + 1) * W] = (numer * lax.rsqrt(mean + 1e-6) * gain_ref[:, columns(j)]).astype(BF)
        if j % PART == PART - 1:
            at = j + 1 - PART
            copy = pltpu.make_async_copy(
                buf.at[:, at * W : (j + 1) * W], out_ref.at[:, columns(at, PART)], sem.at[j // PART]
            )
            copy.start()
            copies.append(copy)
    for copy in copies:
        copy.wait()


def finish_own(core_ref, ld_ref, q_ref, far_inner, carried_ref, gain_ref, out_ref, buf, sem, inner, arrived):
    parts = []
    for p in range(HALF // PART):
        at = slice(p * PART * W, (p + 1) * PART * W)
        parts.append(pltpu.make_async_copy(far_inner.at[:, at], inner.at[:, at], arrived.at[p]))
        parts[p].start()

    def arrive(j):
        if j % PART == 0:
            parts[j // PART].wait()

    finish_half(core_ref, ld_ref, q_ref, inner, carried_ref, gain_ref, out_ref, buf, sem, True, arrive)


def finish_other(core_ref, old_ref, *refs):
    finish_half(core_ref, *refs, False, lambda j: None)


def cost(flops, bytes_accessed):
    return pl.CostEstimate(flops=flops, bytes_accessed=bytes_accessed, transcendentals=0)


def call(kernel, ins, outs, shapes, scratch=(), limit=LIMIT, **kw):
    return pl.pallas_call(
        kernel,
        in_specs=ins,
        out_specs=outs,
        out_shape=shapes,
        scratch_shapes=list(scratch),
        compiler_params=pltpu.CompilerParams(vmem_limit_bytes=limit * MB),
        **kw,
    )


def block_half(kernel, own, which, arrays):
    def group(i, core):
        return (core[0] if own else 1 - core[0]) * (HALF // HB) + i

    return pl.pallas_call(
        kernel,
        grid_spec=pltpu.PrefetchScalarGridSpec(
            num_scalar_prefetch=1,
            grid=(HALF // HB,),
            in_specs=[pl.BlockSpec((HB, T), lambda i, c: (group(i, c), 0))]
            + [pl.BlockSpec((T, HB * W), lambda i, c: (0, group(i, c)))] * 3,
            out_specs=pl.BlockSpec((T, HB * W), lambda i, c: (0, i)),
        ),
        out_shape=pltpu.HBM((T, HALF * W), F32),
        compiler_params=pltpu.CompilerParams(vmem_limit_bytes=LIMIT * MB),
        cost_estimate=cost(1 << 30, 5 * MB),
    )(which, *arrays)


def on_device(queries, keys, values, log_decay, gain):
    which = lax.axis_index("c").astype(jnp.int32).reshape(1)
    heads = log_decay.shape[0]
    chips = HALF * 4
    smem = pl.BlockSpec(memory_space=pltpu.SMEM)
    vmem = pl.BlockSpec(memory_space=pltpu.VMEM)
    hbm = pl.BlockSpec(memory_space=pltpu.HBM)
    struct = jax.ShapeDtypeStruct
    far_q, far_k, far_v, far_ld = (
        pltpu.with_memory_space_constraint(a, pltpu.HBM) for a in (queries, keys, values, log_decay)
    )
    swap = functools.partial(lax.ppermute, axis_name="c", perm=[(0, 1), (1, 0)])
    halves = [
        pltpu.VMEM((T, HALF * W), BF),
        pltpu.VMEM((T, HALF * W), BF),
        pltpu.VMEM((HALF, T), F32),
        pltpu.SemaphoreType.DMA((3,)),
    ]
    sources = (which, far_k, far_v, far_ld)
    sent = call(
        send_states, [smem, hbm, hbm, hbm], vmem, struct((HALF * W + SPLIT, W), BF), halves,
        cost_estimate=cost(1 << 27, 3 * MB),
    )(*sources)
    recv = swap(sent)
    state, decay = call(
        own_states, [smem, hbm, hbm, hbm], [vmem, vmem],
        [struct((HALF, W, W), F32), struct((HALF, W), F32)], halves,
        cost_estimate=cost(1 << 27, 3 * MB),
    )(*sources)
    chunks, first, first_decay = call(
        combine, [smem, vmem, vmem, vmem], [vmem] * 3,
        [struct((chips, ROWS, W), BF), struct((HALF, W, W), BF), struct((HALF, W), F32)],
    )(which, state, decay, recv)
    chunks, far_q = lax.optimization_barrier((chunks, far_q))
    owned = lax.all_to_all(chunks, CHIPS, split_axis=0, concat_axis=0, tiled=True)
    near = block_half(within_half, True, which, (far_ld, far_q, far_k, far_v))
    far = block_half(within_half, False, which, (far_ld, far_q, far_k, far_v))
    owned, near, far = lax.optimization_barrier((owned, near, far))
    before = call(scan_chips, [vmem], vmem, struct((chips, 32, W), BF))(owned)
    back = lax.all_to_all(before, CHIPS, split_axis=0, concat_axis=0, tiled=True)
    keep, give = call(
        spread_back, [smem, vmem, vmem, vmem], [vmem] * 2, [struct((HALF, W, W), BF)] * 2
    )(which, back, first, first_decay)
    taken = swap(give)
    late = (log_decay, queries)
    gains = gain.reshape(1, heads * W)
    out_shape = pltpu.HBM((T, heads * W), BF)
    bufs = [pltpu.VMEM((T, HALF * W), BF), pltpu.SemaphoreType.DMA((HALF // PART,))]
    inner_bufs = [pltpu.VMEM((T, HALF * W), F32), pltpu.SemaphoreType.DMA((HALF // PART,))]
    started = call(
        finish_own, [smem, vmem, vmem, hbm, vmem, vmem], hbm, out_shape, bufs + inner_bufs, FINISH, cost_estimate=cost(1 << 27, 5 * MB)
    )(which, *late, near, keep, gains)
    return call(
        finish_other, [smem, hbm] + [vmem] * 5, hbm, out_shape, bufs, FINISH,
        input_output_aliases={1: 0}, cost_estimate=cost(1 << 27, 5 * MB),
    )(which, started, *late, far, taken, gains)


def solution(mesh):
    chips = Mesh(mesh.devices.reshape(4, 4, 4, 2), ALL)
    placed = (P(ALL, None), P(ALL, None), P(ALL, None), P(None, ALL), P())
    return jax.shard_map(on_device, mesh=chips, in_specs=placed, out_specs=P(ALL, None), check_vma=False)
```

time: 72.7 us -> 60.2 us (0.83)
  blocking collectives: 41.1 us -> 17.8 us
  starting transfers between devices: 4.55 us -> 14.9 us
  waiting for transfers between devices: 0.01 us -> 4.17 us
  local copies, waits for them, and re-layouts: 3.96 us -> 1.6 us
  Pallas kernels: 22.8 us -> 21.3 us
    all_to_all x1 -> x0, blocking collectives: 25.3 us -> none  [on_device(): lax.all_to_all(chunks, CHIPS, split_axis=0, concat_axis=0, tiled=True)]
    all_to_all x0 -> x1, starting transfers between devices: none -> 11.2 us  [on_device(): lax.all_to_all(chunks, CHIPS, split_axis=0, concat_axis=0, tiled=True)]
    all_to_all x0 -> x1, waiting for transfers between devices: none -> 4.16 us  [on_device(): lax.all_to_all(chunks, CHIPS, split_axis=0, concat_axis=0, tiled=True)]
    unnamed x16 -> x10, local copies, waits for them, and re-layouts: 3.96 us -> 1.6 us
    all_to_all x1, blocking collectives: 15.8 us -> 17.8 us  [on_device(): lax.all_to_all(before, CHIPS, split_axis=0, concat_axis=0, tiled=True)]
    pallas_call x8 -> x9, Pallas kernels: 22.8 us -> 21.3 us  [the longest x2 10 us: block_half(): pl.pallas_call(kernel, grid_spec=pltpu.PrefetchScalarGridSpec(num_scalar_...]
    ppermute x1, starting transfers between devices: 3.04 us -> 2.16 us  [on_device(): taken = swap(give)]
  transfers between devices with their start and end apart: 2 -> 3, of which waited for: 0 -> 1; matrix products, arithmetic and copies ran while one was open for 0% -> 0% of each run, Pallas kernels for 22% -> 25%
where the time goes in v3:
time: 60.2 us; the launch traced here: 59.8 us
  Pallas kernels  21.3 us (35%)
  blocking collectives  17.8 us (30%)
  starting transfers between devices  14.9 us (25%)
  waiting for transfers between devices  4.17 us (7%)
  local copies, waits for them, and re-layouts  1.6 us (3%)
    all_to_all x1, blocking collectives, on_device(): lax.all_to_all(before, CHIPS, split_axis=0, concat_axis=0, tiled=True)  17.8 us
    all_to_all x1, starting transfers between devices, on_device(): lax.all_to_all(chunks, CHIPS, split_axis=0, concat_axis=0, tiled=True)  11.2 us
    pallas_call x2, Pallas kernels, block_half(): pl.pallas_call(kernel, grid_spec=pltpu.PrefetchScalarGridSpec(num_scalar_...  10 us
    all_to_all x1, waiting for transfers between devices, on_device(): lax.all_to_all(chunks, CHIPS, split_axis=0, concat_axis=0, tiled=True)  4.16 us
    pallas_call x1, Pallas kernels, on_device(): call(finish_own, [smem, vmem, vmem, hbm, vmem, vmem], hbm, out_shape, buf...  3.04 us
    pallas_call x1, Pallas kernels, on_device(): call(finish_other, [smem, hbm] + [vmem] * 5, hbm, out_shape, bufs, FINISH...  2.39 us
    pallas_call x1, Pallas kernels, on_device(): call(own_states, [smem, hbm, hbm, hbm], [vmem, vmem], [struct((HALF, W, W...  2.18 us
    pallas_call x1, Pallas kernels, on_device(): call(send_states, [smem, hbm, hbm, hbm], vmem, struct((HALF * W + SPLIT,...  2.17 us
  transfers between devices with their start and end apart: 3, of which 1 were waited for; matrix products, arithmetic and copies ran while one was open for 0% of the time, Pallas kernels for 25%

profile of v3, /device:TPU:1, one launch (start us, length us, event | category | flops | bytes accessed | tf_op | source)
XLA Modules:
  0.0 59.8 jit_solution(18106414005452190221)
XLA Ops:
  0.0 2.2 %shard_map.56 = bf16[2096,128]{1,0:T(8,128)(2,1)S(1)} custom-call(s32[1]{0:T(128)} %bitcast.core_ref, bf16[256,4096]{1,0:T(8,128)(2,1)} %refs_2_.3, bf16[256,4096]{1,0:T(8,128)(2,1)} %refs_3_.3, f32[32,256]{1,0:T(8,128)} %refs_0_.5), custom_call_target="tpu_custom_call" | custom-call | flops 134217728 | bytes 3145728 | tf_op jit(solution)/shard_map/pallas_call | solution.py:292
  2.2 1.5 %collective-permute-start = (bf16[2096,128]{1,0:T(8,128)(2,1)S(1)}, bf16[2096,128]{1,0:T(8,128)(2,1)S(1)}, u32[]{:S(2)}, u32[]{:S(2)}) collective-permute-start(bf16[2096,128]{1,0:T(8,128)(2,1)S(1)} %shard_map.56), channel_id=1, source_target_pairs={{0,1},{1,0},{2,3},{3,2},{4,5},{5,4},{6,7},{7,6},{8,9},{9,8},{10,11... | collective-permute-start | bytes 1609736 | tf_op jit(solution)/shard_map/ppermute | solution.py:296
  3.7 2.2 %shard_map.55 = (f32[16,128,128]{2,1,0:T(8,128)S(1)}, f32[16,128]{1,0:T(8,128)S(1)}) custom-call(s32[1]{0:T(128)} %bitcast.core_ref, bf16[256,4096]{1,0:T(8,128)(2,1)} %refs_2_.3, bf16[256,4096]{1,0:T(8,128)(2,1)} %refs_3_.3, f32[32,256]{1,0:T(8,128)} %refs_0_.5), custom_call_target="tpu_custom_call" | custom-call | flops 134217728 | bytes 3145728 | tf_op jit(solution)/shard_map/pallas_call | solution.py:297
  5.9 0.0 collective-permute-done.recv_ref
  5.9 1.1 %shard_map.57 = (bf16[64,40,128]{2,1,0:T(8,128)(2,1)}, bf16[16,128,128]{2,1,0:T(8,128)(2,1)S(1)}, f32[16,128]{1,0:T(8,128)S(1)}) custom-call(s32[1]{0:T(128)} %bitcast.core_ref, f32[16,128,128]{2,1,0:T(8,128)S(1)} %get-tuple-element.17.own_ref, f32[16,128]{1,0:T(8,128)S(1)} %get-tuple-element.18.decay_ref, bf16[2096,128]{1,0:T(8,128)(2,1)S(1)} %collective-permute-done.recv_ref), custom_call_target="tpu_custom_call" | custom-call | tf_op jit(solution)/shard_map/pallas_call | solution.py:302
  6.9 11.2 %all-to-all-start = ((bf16[64,40,128]{2,1,0:T(8,128)(2,1)}), bf16[64,40,128]{2,1,0:T(8,128)(2,1)S(1)}, u32[]{:S(2)}, u32[]{:S(2)}) async-start(bf16[64,40,128]{2,1,0:T(8,128)(2,1)} %get-tuple-element.20), calls=%async_computation | async-start | bytes 1310720 | tf_op jit(solution)/shard_map/all_to_all | solution.py:307
  18.2 5.0 %shard_map.59.refs_2_ = f32[256,2048]{1,0:T(8,128)} custom-call(s32[1]{0:T(128)} %bitcast.core_ref, f32[32,256]{1,0:T(8,128)} %refs_0_.5, bf16[256,4096]{1,0:T(8,128)(2,1)} %refs_1_.3, bf16[256,4096]{1,0:T(8,128)(2,1)} %refs_2_.3, bf16[256,4096]{1,0:T(8,128)(2,1)} %refs_3_.3), custom_call_target="tpu_custom_call" | custom-call | flops 1073741824 | bytes 5242880 | tf_op jit(solution)/shard_map/pallas_call | solution.py:258
  23.2 5.0 %shard_map.58.far_inner = f32[256,2048]{1,0:T(8,128)} custom-call(s32[1]{0:T(128)} %bitcast.core_ref, f32[32,256]{1,0:T(8,128)} %refs_0_.5, bf16[256,4096]{1,0:T(8,128)(2,1)} %refs_1_.3, bf16[256,4096]{1,0:T(8,128)(2,1)} %refs_2_.3, bf16[256,4096]{1,0:T(8,128)(2,1)} %refs_3_.3), custom_call_target="tpu_custom_call" | custom-call | flops 1073741824 | bytes 5242880 | tf_op jit(solution)/shard_map/pallas_call | solution.py:258
  28.2 0.0 copy-start
  28.2 0.0 copy-start.3
  28.2 0.0 copy-start.4
  28.2 4.2 %all-to-all-done.in_ref = bf16[64,40,128]{2,1,0:T(8,128)(2,1)S(1)} async-done(((bf16[64,40,128]{2,1,0:T(8,128)(2,1)}), bf16[64,40,128]{2,1,0:T(8,128)(2,1)S(1)}, u32[]{:S(2)}, u32[]{:S(2)}) %all-to-all-start) | async-done | bytes 655392 | tf_op jit(solution)/shard_map/all_to_all | solution.py:307
  32.3 0.2 shard_map.60
  32.5 17.8 %all_to_all.10.chip_ref = bf16[64,32,128]{2,1,0:T(8,128)(2,1)S(1)} all-to-all(bf16[64,32,128]{2,1,0:T(8,128)(2,1)S(1)} %shard_map.60), channel_id=1, replica_groups=mesh['z'=4,'y'=4,'x'=4,'c'=2] {'z','y','x'}, dimensions={0} | all-to-all | bytes 1048576 | tf_op jit(solution)/shard_map/all_to_all | solution.py:312
  50.3 0.3 shard_map.61
  50.6 2.2 %collective-permute-start.1 = (bf16[16,128,128]{2,1,0:T(8,128)(2,1)S(1)}, bf16[16,128,128]{2,1,0:T(8,128)(2,1)S(1)}, u32[]{:S(2)}, u32[]{:S(2)}) collective-permute-start(bf16[16,128,128]{2,1,0:T(8,128)(2,1)S(1)} %get-tuple-element.28), channel_id=1, source_target_pairs={{0,1},{1,0},{2,3},{3,2},{4,5},{5,4},{6,7},{7,6},{8,9},{9,8},{10,11... | collective-permute-start | bytes 1572872 | tf_op jit(solution)/shard_map/ppermute | solution.py:316
  52.7 0.0 copy-done
  52.7 0.0 copy-done.3
  52.7 0.0 copy-done.4
  52.7 0.0 copy-start.2
  52.7 1.6 %copy-done.2 = f32[256,2048]{1,0:T(8,128)S(1)} copy-done((f32[256,2048]{1,0:T(8,128)S(1)}, f32[256,2048]{1,0:T(8,128)}, u32[]{:S(2)}) %copy-start.2) | copy-done | bytes 2097176
  54.3 0.0 copy-start.1
  54.3 3.0 %shard_map.62.old_ref = bf16[256,4096]{1,0:T(8,128)(2,1)} custom-call(s32[1]{0:T(128)} %bitcast.core_ref, f32[32,256]{1,0:T(8,128)S(1)} %copy-done.3, bf16[256,4096]{1,0:T(8,128)(2,1)S(1)} %copy-done, f32[256,2048]{1,0:T(8,128)S(1)} %copy-done.2, bf16[16,128,128]{2,1,0:T(8,128)(2,1)S(1)} %get-tuple-element.26.carried_ref, f32[1,4096]{1,0:T(1,128)S(1)} %bitcast.2), custom_call_target="tpu_custom_call" | custom-call | flops 134217728 | bytes 5242880 | tf_op jit(solution)/shard_map/pallas_call | solution.py:322
  57.4 0.0 collective-permute-done.1.refs_3_
  57.4 0.0 copy-done.1
  57.4 2.4 %shard_map.63 = bf16[256,4096]{1,0:T(8,128)(2,1)} custom-call(s32[1]{0:T(128)} %bitcast.core_ref, bf16[256,4096]{1,0:T(8,128)(2,1)} %shard_map.62.old_ref, f32[32,256]{1,0:T(8,128)S(1)} %copy-done.3, bf16[256,4096]{1,0:T(8,128)(2,1)S(1)} %copy-done, f32[256,2048]{1,0:T(8,128)S(1)} %copy-done.1, ...), custom_call_target="tpu_custom_call", output_to_operand_aliasing={{}: (1, {})} | custom-call | flops 134217728 | bytes 5242880 | tf_op jit(solution)/shard_map/pallas_call | solution.py:325
Async XLA Ops:
  2.2 3.7 %collective-permute-start = (bf16[2096,128]{1,0:T(8,128)(2,1)S(1)}, bf16[2096,128]{1,0:T(8,128)(2,1)S(1)}, u32[]{:S(2)}, u32[]{:S(2)}) collective-permute-start(bf16[2096,128]{1,0:T(8,128)(2,1)S(1)} %shard_map.56), channel_id=1, source_target_pairs={{0,1},{1,0},{2,3},{3,2},{4,5},{5,4},{6,7},{7,6},{8,9},{9,8},{10,11... | collective-permute-start | bytes 1609736 | tf_op jit(solution)/shard_map/ppermute | solution.py:296
  6.9 25.4 %all-to-all-start = ((bf16[64,40,128]{2,1,0:T(8,128)(2,1)}), bf16[64,40,128]{2,1,0:T(8,128)(2,1)S(1)}, u32[]{:S(2)}, u32[]{:S(2)}) async-start(bf16[64,40,128]{2,1,0:T(8,128)(2,1)} %get-tuple-element.20), calls=%async_computation | async-start | bytes 1310720 | tf_op jit(solution)/shard_map/all_to_all | solution.py:307
  28.2 24.6 %copy-start = (bf16[256,4096]{1,0:T(8,128)(2,1)S(1)}, bf16[256,4096]{1,0:T(8,128)(2,1)}, u32[]{:S(2)}) copy-start(bf16[256,4096]{1,0:T(8,128)(2,1)} %refs_1_.3) | copy-start | bytes 6291460
  28.2 24.6 %copy-start.3 = (f32[32,256]{1,0:T(8,128)S(1)}, f32[32,256]{1,0:T(8,128)}, u32[]{:S(2)}) copy-start(f32[32,256]{1,0:T(8,128)} %refs_0_.5) | copy-start | bytes 98308
  28.2 24.6 %copy-start.4 = (f32[4096]{0:T(1024)S(1)}, f32[4096]{0:T(1024)}, u32[]{:S(2)}) copy-start(f32[4096]{0:T(1024)} %param.9) | copy-start | bytes 49156
  50.6 6.8 %collective-permute-start.1 = (bf16[16,128,128]{2,1,0:T(8,128)(2,1)S(1)}, bf16[16,128,128]{2,1,0:T(8,128)(2,1)S(1)}, u32[]{:S(2)}, u32[]{:S(2)}) collective-permute-start(bf16[16,128,128]{2,1,0:T(8,128)(2,1)S(1)} %get-tuple-element.28), channel_id=1, source_target_pairs={{0,1},{1,0},{2,3},{3,2},{4,5},{5,4},{6,7},{7,6},{8,9},{9,8},{10,11... | collective-permute-start | bytes 1572872 | tf_op jit(solution)/shard_map/ppermute | solution.py:316
  52.7 1.6 %copy-start.2 = (f32[256,2048]{1,0:T(8,128)S(1)}, f32[256,2048]{1,0:T(8,128)}, u32[]{:S(2)}) copy-start(f32[256,2048]{1,0:T(8,128)} %shard_map.58.far_inner) | copy-start | bytes 6291460
  54.3 3.1 %copy-start.1 = (f32[256,2048]{1,0:T(8,128)S(1)}, f32[256,2048]{1,0:T(8,128)}, u32[]{:S(2)}) copy-start(f32[256,2048]{1,0:T(8,128)} %shard_map.59.refs_2_) | copy-start | bytes 6291460

commit v4 on v3

--- a/solution.py
+++ b/solution.py
@@ -18,6 +18,7 @@
 HALF = 16
 SPLIT = 48
 ROWS = 40
+AHEAD = 1
 PART = 4
 MB = 1 << 20
 LIMIT = 12
@@ -140,7 +141,7 @@
             send_ref[h, rows, :] = jnp.where(earlier, second, first).astype(BF)
 
 
-def within(ld_ref, q_ref, k_ref, v_ref, out_ref):
+def within(core_ref, ld_ref, q_ref, k_ref, v_ref, out_ref):
     cum = running(ld_ref[...])
     cols = cum.T
     n = W
@@ -181,43 +182,28 @@
     total(HB - 1, *waiting)
 
 
-def within_half(core_ref, *refs):
-    within(*refs)
-
-
-def finish_half(core_ref, ld_ref, q_ref, inner_ref, carried_ref, gain_ref, out_ref, buf, sem, own, arrive):
-    half = core_ref[0] if own else 1 - core_ref[0]
+def finish_half(half, ld_ref, q_ref, inner_ref, carried_ref, gain_ref, put, arrive, skip):
     grown = jnp.exp(running(ld_ref[pl.ds(pl.multiple_of(half * HALF, HALF), HALF), :])).T
     ones = jnp.full((W, W), 1.0 / W, BF)
 
-    def columns(j, count=1):
-        return pl.ds(pl.multiple_of(half * HALF * W + j * W, W), count * W)
+    def columns(j):
+        return pl.ds(pl.multiple_of(half * HALF * W + j * W, W), W)
 
     def readout(j):
         return dot(q_ref[:, columns(j)], carried_ref[j])
 
-    copies = []
-    following = readout(0)
+    ready = [readout(j) for j in range(AHEAD)]
     for j in range(HALF):
-        current = following
-        if j + 1 < HALF:
-            following = readout(j + 1)
+        if j + AHEAD < HALF:
+            ready.append(readout(j + AHEAD))
         arrive(j)
-        numer = inner_ref[:, j * W : (j + 1) * W] + current * grown[:, j : j + 1]
+        at = slice((skip + j) * W, (skip + j + 1) * W)
+        numer = inner_ref[:, at] + ready[j] * grown[:, j : j + 1]
         mean = dot((numer * numer).astype(BF), ones)
-        buf[:, j * W : (j + 1) * W] = (numer * lax.rsqrt(mean + 1e-6) * gain_ref[:, columns(j)]).astype(BF)
-        if j % PART == PART - 1:
-            at = j + 1 - PART
-            copy = pltpu.make_async_copy(
-                buf.at[:, at * W : (j + 1) * W], out_ref.at[:, columns(at, PART)], sem.at[j // PART]
-            )
-            copy.start()
-            copies.append(copy)
-    for copy in copies:
-        copy.wait()
-
-
-def finish_own(core_ref, ld_ref, q_ref, far_inner, carried_ref, gain_ref, out_ref, buf, sem, inner, arrived):
+        put(j, (numer * lax.rsqrt(mean + 1e-6) * gain_ref[:, columns(j)]).astype(BF))
+
+
+def finish_own(core_ref, ld_ref, q_ref, far_inner, carried_ref, gain_ref, out_ref, inner, arrived):
     parts = []
     for p in range(HALF // PART):
         at = slice(p * PART * W, (p + 1) * PART * W)
@@ -228,11 +214,30 @@
         if j % PART == 0:
             parts[j // PART].wait()
 
-    finish_half(core_ref, ld_ref, q_ref, inner, carried_ref, gain_ref, out_ref, buf, sem, True, arrive)
-
-
-def finish_other(core_ref, old_ref, *refs):
-    finish_half(core_ref, *refs, False, lambda j: None)
+    def put(j, value):
+        out_ref[:, j * W : (j + 1) * W] = value
+
+    finish_half(core_ref[0], ld_ref, q_ref, inner, carried_ref, gain_ref, put, arrive, 0)
+
+
+def finish_other(core_ref, own_ref, ld_ref, q_ref, inner_ref, carried_ref, gain_ref, out_ref, buf, sem):
+    half = 1 - core_ref[0]
+    first = pl.ds(pl.multiple_of(core_ref[0] * HALF * W, HALF * W), HALF * W)
+    copies = [pltpu.make_async_copy(own_ref, out_ref.at[:, first], sem.at[HALF // PART])]
+    copies[0].start()
+
+    def put(j, value):
+        buf[:, j * W : (j + 1) * W] = value
+        if j % PART == PART - 1:
+            at = j + 1 - PART
+            to = pl.ds(pl.multiple_of(half * HALF * W + at * W, W), PART * W)
+            copy = pltpu.make_async_copy(buf.at[:, at * W : (j + 1) * W], out_ref.at[:, to], sem.at[j // PART])
+            copy.start()
+            copies.append(copy)
+
+    finish_half(half, ld_ref, q_ref, inner_ref, carried_ref, gain_ref, put, lambda j: None, HALF)
+    for copy in copies:
+        copy.wait()
 
 
 def cost(flops, bytes_accessed):
@@ -251,22 +256,24 @@
     )
 
 
-def block_half(kernel, own, which, arrays):
+def within_blocks(which, *arrays):
+    groups = 2 * HALF // HB
+
     def group(i, core):
-        return (core[0] if own else 1 - core[0]) * (HALF // HB) + i
+        return (core[0] * (HALF // HB) + i) % groups
 
     return pl.pallas_call(
-        kernel,
+        within,
         grid_spec=pltpu.PrefetchScalarGridSpec(
             num_scalar_prefetch=1,
-            grid=(HALF // HB,),
+            grid=(groups,),
             in_specs=[pl.BlockSpec((HB, T), lambda i, c: (group(i, c), 0))]
             + [pl.BlockSpec((T, HB * W), lambda i, c: (0, group(i, c)))] * 3,
             out_specs=pl.BlockSpec((T, HB * W), lambda i, c: (0, i)),
         ),
-        out_shape=pltpu.HBM((T, HALF * W), F32),
+        out_shape=pltpu.HBM((T, groups * HB * W), F32),
         compiler_params=pltpu.CompilerParams(vmem_limit_bytes=LIMIT * MB),
-        cost_estimate=cost(1 << 30, 5 * MB),
+        cost_estimate=cost(1 << 31, 10 * MB),
     )(which, *arrays)
 
 
@@ -305,27 +312,25 @@
     )(which, state, decay, recv)
     chunks, far_q = lax.optimization_barrier((chunks, far_q))
     owned = lax.all_to_all(chunks, CHIPS, split_axis=0, concat_axis=0, tiled=True)
-    near = block_half(within_half, True, which, (far_ld, far_q, far_k, far_v))
-    far = block_half(within_half, False, which, (far_ld, far_q, far_k, far_v))
-    owned, near, far = lax.optimization_barrier((owned, near, far))
+    inner = within_blocks(which, far_ld, far_q, far_k, far_v)
+    owned, inner = lax.optimization_barrier((owned, inner))
     before = call(scan_chips, [vmem], vmem, struct((chips, 32, W), BF))(owned)
     back = lax.all_to_all(before, CHIPS, split_axis=0, concat_axis=0, tiled=True)
     keep, give = call(
         spread_back, [smem, vmem, vmem, vmem], [vmem] * 2, [struct((HALF, W, W), BF)] * 2
     )(which, back, first, first_decay)
     taken = swap(give)
-    late = (log_decay, queries)
     gains = gain.reshape(1, heads * W)
-    out_shape = pltpu.HBM((T, heads * W), BF)
-    bufs = [pltpu.VMEM((T, HALF * W), BF), pltpu.SemaphoreType.DMA((HALF // PART,))]
-    inner_bufs = [pltpu.VMEM((T, HALF * W), F32), pltpu.SemaphoreType.DMA((HALF // PART,))]
     started = call(
-        finish_own, [smem, vmem, vmem, hbm, vmem, vmem], hbm, out_shape, bufs + inner_bufs, FINISH, cost_estimate=cost(1 << 27, 5 * MB)
-    )(which, *late, near, keep, gains)
+        finish_own, [smem, vmem, vmem, hbm, vmem, vmem], vmem, struct((T, HALF * W), BF),
+        [pltpu.VMEM((T, HALF * W), F32), pltpu.SemaphoreType.DMA((HALF // PART,))], FINISH,
+        cost_estimate=cost(1 << 27, 5 * MB),
+    )(which, log_decay, queries, pltpu.with_memory_space_constraint(inner, pltpu.HBM), keep, gains)
     return call(
-        finish_other, [smem, hbm] + [vmem] * 5, hbm, out_shape, bufs, FINISH,
-        input_output_aliases={1: 0}, cost_estimate=cost(1 << 27, 5 * MB),
-    )(which, started, *late, far, taken, gains)
+        finish_other, [smem] + [vmem] * 6, hbm, pltpu.HBM((T, heads * W), BF),
+        [pltpu.VMEM((T, HALF * W), BF), pltpu.SemaphoreType.DMA((HALF // PART + 1,))], FINISH,
+        cost_estimate=cost(1 << 27, 5 * MB),
+    )(which, started, log_decay, queries, inner, taken, gains)
 
 
 def solution(mesh):

time: 60.2 us -> 57 us (0.947)
  blocking collectives: 17.8 us -> 15.5 us
  Pallas kernels: 21.3 us -> 19.1 us
  waiting for transfers between devices: 4.17 us -> 5.99 us
  local copies, waits for them, and re-layouts: 1.6 us -> 0.13 us
  starting transfers between devices: 14.9 us -> 15.8 us
    all_to_all x1, blocking collectives: 17.8 us -> 15.5 us  [on_device(): lax.all_to_all(before, CHIPS, split_axis=0, concat_axis=0, tiled=True)]
    pallas_call x4 -> x3, Pallas kernels: 15.4 us -> 13.3 us  [the longest x1 8.19 us: within_blocks(): pl.pallas_call(within, grid_spec=pltpu.PrefetchScalarGridSpec(num_scalar_...]
    all_to_all x1, waiting for transfers between devices: 4.16 us -> 5.98 us  [on_device(): lax.all_to_all(chunks, CHIPS, split_axis=0, concat_axis=0, tiled=True)]
    unnamed x10 -> x8, local copies, waits for them, and re-layouts: 1.6 us -> 0.13 us
    ppermute x1, starting transfers between devices: 2.16 us -> 3.04 us  [on_device(): taken = swap(give)]
  transfers between devices with their start and end apart: 3 -> 3, of which waited for: 1 -> 1; matrix products, arithmetic and copies ran while one was open for 0% -> 0% of each run, Pallas kernels for 25% -> 23%
where the time goes in v4:
time: 57 us; the launch traced here: 56.6 us
  Pallas kernels  19.1 us (34%)
  starting transfers between devices  15.8 us (28%)
  blocking collectives  15.5 us (27%)
  waiting for transfers between devices  5.99 us (11%)
    all_to_all x1, blocking collectives, on_device(): lax.all_to_all(before, CHIPS, split_axis=0, concat_axis=0, tiled=True)  15.5 us
    all_to_all x1, starting transfers between devices, on_device(): lax.all_to_all(chunks, CHIPS, split_axis=0, concat_axis=0, tiled=True)  11.2 us
    pallas_call x1, Pallas kernels, within_blocks(): pl.pallas_call(within, grid_spec=pltpu.PrefetchScalarGridSpec(num_scalar_...  8.19 us
    all_to_all x1, waiting for transfers between devices, on_device(): lax.all_to_all(chunks, CHIPS, split_axis=0, concat_axis=0, tiled=True)  5.98 us
    ppermute x1, starting transfers between devices, on_device(): taken = swap(give)  3.04 us
    pallas_call x1, Pallas kernels, on_device(): call(finish_own, [smem, vmem, vmem, hbm, vmem, vmem], vmem, struct((T, HA...  2.68 us
    pallas_call x1, Pallas kernels, on_device(): call(finish_other, [smem] + [vmem] * 6, hbm, pltpu.HBM((T, heads * W), BF...  2.42 us
    pallas_call x1, Pallas kernels, on_device(): call(own_states, [smem, hbm, hbm, hbm], [vmem, vmem], [struct((HALF, W, W...  2.18 us
  transfers between devices with their start and end apart: 3, of which 1 were waited for; matrix products, arithmetic and copies ran while one was open for 0% of the time, Pallas kernels for 23%

profile of v4, /device:TPU:1, one launch (start us, length us, event | category | flops | bytes accessed | tf_op | source)
XLA Modules:
  0.0 56.6 jit_solution(10812153708558607341)
XLA Ops:
  0.0 2.2 %shard_map.56 = bf16[2096,128]{1,0:T(8,128)(2,1)S(1)} custom-call(s32[1]{0:T(128)} %bitcast.core_ref, bf16[256,4096]{1,0:T(8,128)(2,1)} %k_ref.5, bf16[256,4096]{1,0:T(8,128)(2,1)} %v_ref.5, f32[32,256]{1,0:T(8,128)} %ld_ref.9), custom_call_target="tpu_custom_call" | custom-call | flops 134217728 | bytes 3145728 | tf_op jit(solution)/shard_map/pallas_call | solution.py:299
  2.2 1.5 %collective-permute-start = (bf16[2096,128]{1,0:T(8,128)(2,1)S(1)}, bf16[2096,128]{1,0:T(8,128)(2,1)S(1)}, u32[]{:S(2)}, u32[]{:S(2)}) collective-permute-start(bf16[2096,128]{1,0:T(8,128)(2,1)S(1)} %shard_map.56), channel_id=1, source_target_pairs={{0,1},{1,0},{2,3},{3,2},{4,5},{5,4},{6,7},{7,6},{8,9},{9,8},{10,11... | collective-permute-start | bytes 1609736 | tf_op jit(solution)/shard_map/ppermute | solution.py:303
  3.7 2.2 %shard_map.55 = (f32[16,128,128]{2,1,0:T(8,128)S(1)}, f32[16,128]{1,0:T(8,128)S(1)}) custom-call(s32[1]{0:T(128)} %bitcast.core_ref, bf16[256,4096]{1,0:T(8,128)(2,1)} %k_ref.5, bf16[256,4096]{1,0:T(8,128)(2,1)} %v_ref.5, f32[32,256]{1,0:T(8,128)} %ld_ref.9), custom_call_target="tpu_custom_call" | custom-call | flops 134217728 | bytes 3145728 | tf_op jit(solution)/shard_map/pallas_call | solution.py:304
  5.9 0.0 collective-permute-done.recv_ref
  5.9 1.0 %shard_map.57 = (bf16[64,40,128]{2,1,0:T(8,128)(2,1)}, bf16[16,128,128]{2,1,0:T(8,128)(2,1)S(1)}, f32[16,128]{1,0:T(8,128)S(1)}) custom-call(s32[1]{0:T(128)} %bitcast.core_ref, f32[16,128,128]{2,1,0:T(8,128)S(1)} %get-tuple-element.16.own_ref, f32[16,128]{1,0:T(8,128)S(1)} %get-tuple-element.17.decay_ref, bf16[2096,128]{1,0:T(8,128)(2,1)S(1)} %collective-permute-done.recv_ref), custom_call_target="tpu_custom_call" | custom-call | tf_op jit(solution)/shard_map/pallas_call | solution.py:309
  6.9 11.2 %all-to-all-start = ((bf16[64,40,128]{2,1,0:T(8,128)(2,1)}), bf16[64,40,128]{2,1,0:T(8,128)(2,1)S(1)}, u32[]{:S(2)}, u32[]{:S(2)}) async-start(bf16[64,40,128]{2,1,0:T(8,128)(2,1)} %get-tuple-element.19), calls=%async_computation | async-start | bytes 1310720 | tf_op jit(solution)/shard_map/all_to_all | solution.py:314
  18.1 8.2 %shard_map.58.far_inner.inner_ref = f32[256,4096]{1,0:T(8,128)} custom-call(s32[1]{0:T(128)} %bitcast.core_ref, f32[32,256]{1,0:T(8,128)} %ld_ref.9, bf16[256,4096]{1,0:T(8,128)(2,1)} %q_ref.4, bf16[256,4096]{1,0:T(8,128)(2,1)} %k_ref.5, bf16[256,4096]{1,0:T(8,128)(2,1)} %v_ref.5), custom_call_target="tpu_custom_call" | custom-call | flops 2147483648 | bytes 10485760 | tf_op jit(solution)/shard_map/pallas_call | solution.py:265
  26.3 0.0 copy-start.1
  26.3 0.0 copy-start.2
  26.3 0.0 copy-start.3
  26.3 6.0 %all-to-all-done.in_ref = bf16[64,40,128]{2,1,0:T(8,128)(2,1)S(1)} async-done(((bf16[64,40,128]{2,1,0:T(8,128)(2,1)}), bf16[64,40,128]{2,1,0:T(8,128)(2,1)S(1)}, u32[]{:S(2)}, u32[]{:S(2)}) %all-to-all-start) | async-done | bytes 655392 | tf_op jit(solution)/shard_map/all_to_all | solution.py:314
  32.3 0.2 shard_map.59
  32.5 15.5 %all_to_all.10.chip_ref = bf16[64,32,128]{2,1,0:T(8,128)(2,1)S(1)} all-to-all(bf16[64,32,128]{2,1,0:T(8,128)(2,1)S(1)} %shard_map.59), channel_id=1, replica_groups=mesh['z'=4,'y'=4,'x'=4,'c'=2] {'z','y','x'}, dimensions={0} | all-to-all | bytes 1048576 | tf_op jit(solution)/shard_map/all_to_all | solution.py:318
  48.0 0.3 shard_map.60
  48.3 3.0 %collective-permute-start.1 = (bf16[16,128,128]{2,1,0:T(8,128)(2,1)S(1)}, bf16[16,128,128]{2,1,0:T(8,128)(2,1)S(1)}, u32[]{:S(2)}, u32[]{:S(2)}) collective-permute-start(bf16[16,128,128]{2,1,0:T(8,128)(2,1)S(1)} %get-tuple-element.26), channel_id=1, source_target_pairs={{0,1},{1,0},{2,3},{3,2},{4,5},{5,4},{6,7},{7,6},{8,9},{9,8},{10,11... | collective-permute-start | bytes 1572872 | tf_op jit(solution)/shard_map/ppermute | solution.py:322
  51.3 0.0 copy-done.1
  51.3 0.0 copy-done.2
  51.3 0.0 copy-done.3
  51.3 0.0 copy-start
  51.3 2.7 %shard_map.61.own_ref = bf16[256,2048]{1,0:T(8,128)(2,1)S(1)} custom-call(s32[1]{0:T(128)} %bitcast.core_ref, f32[32,256]{1,0:T(8,128)S(1)} %copy-done.2, bf16[256,4096]{1,0:T(8,128)(2,1)S(1)} %copy-done.1, f32[256,4096]{1,0:T(8,128)} %shard_map.58.far_inner.inner_ref, bf16[16,128,128]{2,1,0:T(8,128)(2,1)S(1)} %get-tuple-element.25.carried_ref, ...), custom_call_target="tpu_custom_call" | custom-call | flops 134217728 | bytes 5242880 | tf_op jit(solution)/shard_map/pallas_call | solution.py:324
  54.0 0.0 collective-permute-done.1.carried_ref
  54.0 0.1 copy-done
  54.1 2.4 %shard_map.62 = bf16[256,4096]{1,0:T(8,128)(2,1)} custom-call(s32[1]{0:T(128)} %bitcast.core_ref, bf16[256,2048]{1,0:T(8,128)(2,1)S(1)} %shard_map.61.own_ref, f32[32,256]{1,0:T(8,128)S(1)} %copy-done.2, bf16[256,4096]{1,0:T(8,128)(2,1)S(1)} %copy-done.1, f32[256,4096]{1,0:T(8,128)S(1)} %copy-done, ...), custom_call_target="tpu_custom_call" | custom-call | flops 134217728 | bytes 5242880 | tf_op jit(solution)/shard_map/pallas_call | solution.py:329
Async XLA Ops:
  2.2 3.7 %collective-permute-start = (bf16[2096,128]{1,0:T(8,128)(2,1)S(1)}, bf16[2096,128]{1,0:T(8,128)(2,1)S(1)}, u32[]{:S(2)}, u32[]{:S(2)}) collective-permute-start(bf16[2096,128]{1,0:T(8,128)(2,1)S(1)} %shard_map.56), channel_id=1, source_target_pairs={{0,1},{1,0},{2,3},{3,2},{4,5},{5,4},{6,7},{7,6},{8,9},{9,8},{10,11... | collective-permute-start | bytes 1609736 | tf_op jit(solution)/shard_map/ppermute | solution.py:303
  6.9 25.4 %all-to-all-start = ((bf16[64,40,128]{2,1,0:T(8,128)(2,1)}), bf16[64,40,128]{2,1,0:T(8,128)(2,1)S(1)}, u32[]{:S(2)}, u32[]{:S(2)}) async-start(bf16[64,40,128]{2,1,0:T(8,128)(2,1)} %get-tuple-element.19), calls=%async_computation | async-start | bytes 1310720 | tf_op jit(solution)/shard_map/all_to_all | solution.py:314
  26.3 25.0 %copy-start.1 = (bf16[256,4096]{1,0:T(8,128)(2,1)S(1)}, bf16[256,4096]{1,0:T(8,128)(2,1)}, u32[]{:S(2)}) copy-start(bf16[256,4096]{1,0:T(8,128)(2,1)} %q_ref.4) | copy-start | bytes 6291460
  26.3 25.0 %copy-start.2 = (f32[32,256]{1,0:T(8,128)S(1)}, f32[32,256]{1,0:T(8,128)}, u32[]{:S(2)}) copy-start(f32[32,256]{1,0:T(8,128)} %ld_ref.9) | copy-start | bytes 98308
  26.3 25.0 %copy-start.3 = (f32[4096]{0:T(1024)S(1)}, f32[4096]{0:T(1024)}, u32[]{:S(2)}) copy-start(f32[4096]{0:T(1024)} %param.9) | copy-start | bytes 49156
  48.3 5.8 %collective-permute-start.1 = (bf16[16,128,128]{2,1,0:T(8,128)(2,1)S(1)}, bf16[16,128,128]{2,1,0:T(8,128)(2,1)S(1)}, u32[]{:S(2)}, u32[]{:S(2)}) collective-permute-start(bf16[16,128,128]{2,1,0:T(8,128)(2,1)S(1)} %get-tuple-element.26), channel_id=1, source_target_pairs={{0,1},{1,0},{2,3},{3,2},{4,5},{5,4},{6,7},{7,6},{8,9},{9,8},{10,11... | collective-permute-start | bytes 1572872 | tf_op jit(solution)/shard_map/ppermute | solution.py:322
  51.3 2.8 %copy-start = (f32[256,4096]{1,0:T(8,128)S(1)}, f32[256,4096]{1,0:T(8,128)}, u32[]{:S(2)}) copy-start(f32[256,4096]{1,0:T(8,128)} %shard_map.58.far_inner.inner_ref) | copy-start | bytes 12582916

commit v5 on v4

--- a/solution.py
+++ b/solution.py
@@ -129,7 +129,7 @@
         carry = decay * carry + x[:32]
 
 
-def spread_back(core_ref, chip_ref, first_ref, first_decay_ref, keep_ref, send_ref):
+def spread_back(core_ref, near_ref, chip_ref, first_ref, first_decay_ref, keep_ref, send_ref):
     earlier = core_ref[0] == 0
     decay = first_decay_ref[...]
     for h in range(HALF):
@@ -141,7 +141,17 @@
             send_ref[h, rows, :] = jnp.where(earlier, second, first).astype(BF)
 
 
-def within(core_ref, ld_ref, q_ref, k_ref, v_ref, out_ref):
+def within(core_ref, ld_ref, q_ref, k_ref, v_ref, near_ref, far_ref):
+    @pl.when(pl.program_id(0) < HALF // HB)
+    def _():
+        within_step(ld_ref, q_ref, k_ref, v_ref, near_ref)
+
+    @pl.when(pl.program_id(0) >= HALF // HB)
+    def _():
+        within_step(ld_ref, q_ref, k_ref, v_ref, far_ref)
+
+
+def within_step(ld_ref, q_ref, k_ref, v_ref, out_ref):
     cum = running(ld_ref[...])
     cols = cum.T
     n = W
@@ -182,7 +192,7 @@
     total(HB - 1, *waiting)
 
 
-def finish_half(half, ld_ref, q_ref, inner_ref, carried_ref, gain_ref, put, arrive, skip):
+def finish_half(half, ld_ref, q_ref, inner_ref, carried_ref, gain_ref, put):
     grown = jnp.exp(running(ld_ref[pl.ds(pl.multiple_of(half * HALF, HALF), HALF), :])).T
     ones = jnp.full((W, W), 1.0 / W, BF)
 
@@ -196,28 +206,17 @@
     for j in range(HALF):
         if j + AHEAD < HALF:
             ready.append(readout(j + AHEAD))
-        arrive(j)
-        at = slice((skip + j) * W, (skip + j + 1) * W)
+        at = slice(j * W, (j + 1) * W)
         numer = inner_ref[:, at] + ready[j] * grown[:, j : j + 1]
         mean = dot((numer * numer).astype(BF), ones)
         put(j, (numer * lax.rsqrt(mean + 1e-6) * gain_ref[:, columns(j)]).astype(BF))
 
 
-def finish_own(core_ref, ld_ref, q_ref, far_inner, carried_ref, gain_ref, out_ref, inner, arrived):
-    parts = []
-    for p in range(HALF // PART):
-        at = slice(p * PART * W, (p + 1) * PART * W)
-        parts.append(pltpu.make_async_copy(far_inner.at[:, at], inner.at[:, at], arrived.at[p]))
-        parts[p].start()
-
-    def arrive(j):
-        if j % PART == 0:
-            parts[j // PART].wait()
-
+def finish_own(core_ref, ld_ref, q_ref, inner_ref, carried_ref, gain_ref, out_ref):
     def put(j, value):
         out_ref[:, j * W : (j + 1) * W] = value
 
-    finish_half(core_ref[0], ld_ref, q_ref, inner, carried_ref, gain_ref, put, arrive, 0)
+    finish_half(core_ref[0], ld_ref, q_ref, inner_ref, carried_ref, gain_ref, put)
 
 
 def finish_other(core_ref, own_ref, ld_ref, q_ref, inner_ref, carried_ref, gain_ref, out_ref, buf, sem):
@@ -235,7 +234,7 @@
             copy.start()
             copies.append(copy)
 
-    finish_half(half, ld_ref, q_ref, inner_ref, carried_ref, gain_ref, put, lambda j: None, HALF)
+    finish_half(half, ld_ref, q_ref, inner_ref, carried_ref, gain_ref, put)
     for copy in copies:
         copy.wait()
 
@@ -269,9 +268,12 @@
             grid=(groups,),
             in_specs=[pl.BlockSpec((HB, T), lambda i, c: (group(i, c), 0))]
             + [pl.BlockSpec((T, HB * W), lambda i, c: (0, group(i, c)))] * 3,
-            out_specs=pl.BlockSpec((T, HB * W), lambda i, c: (0, i)),
+            out_specs=[
+                pl.BlockSpec((T, HB * W), lambda i, c: (0, jnp.minimum(i, groups // 2 - 1))),
+                pl.BlockSpec((T, HB * W), lambda i, c: (0, jnp.maximum(i - groups // 2, 0))),
+            ],
         ),
-        out_shape=pltpu.HBM((T, groups * HB * W), F32),
+        out_shape=[pltpu.HBM((T, HALF * W), F32)] * 2,
         compiler_params=pltpu.CompilerParams(vmem_limit_bytes=LIMIT * MB),
         cost_estimate=cost(1 << 31, 10 * MB),
     )(which, *arrays)
@@ -312,25 +314,25 @@
     )(which, state, decay, recv)
     chunks, far_q = lax.optimization_barrier((chunks, far_q))
     owned = lax.all_to_all(chunks, CHIPS, split_axis=0, concat_axis=0, tiled=True)
-    inner = within_blocks(which, far_ld, far_q, far_k, far_v)
-    owned, inner = lax.optimization_barrier((owned, inner))
-    before = call(scan_chips, [vmem], vmem, struct((chips, 32, W), BF))(owned)
+    near, far = within_blocks(which, far_ld, far_q, far_k, far_v)
+    owned, near, far = lax.optimization_barrier((owned, near, far))
+    before = call(scan_chips, [vmem], vmem, struct((chips, 32, W), BF), cost_estimate=cost(1 << 10, 1 << 10))(owned)
     back = lax.all_to_all(before, CHIPS, split_axis=0, concat_axis=0, tiled=True)
     keep, give = call(
-        spread_back, [smem, vmem, vmem, vmem], [vmem] * 2, [struct((HALF, W, W), BF)] * 2
-    )(which, back, first, first_decay)
+        spread_back, [smem, vmem, vmem, vmem, vmem], [vmem] * 2, [struct((HALF, W, W), BF)] * 2,
+        cost_estimate=cost(1 << 10, 1 << 10),
+    )(which, near, back, first, first_decay)
     taken = swap(give)
     gains = gain.reshape(1, heads * W)
     started = call(
-        finish_own, [smem, vmem, vmem, hbm, vmem, vmem], vmem, struct((T, HALF * W), BF),
-        [pltpu.VMEM((T, HALF * W), F32), pltpu.SemaphoreType.DMA((HALF // PART,))], FINISH,
+        finish_own, [smem] + [vmem] * 5, vmem, struct((T, HALF * W), BF), limit=FINISH,
         cost_estimate=cost(1 << 27, 5 * MB),
-    )(which, log_decay, queries, pltpu.with_memory_space_constraint(inner, pltpu.HBM), keep, gains)
+    )(which, log_decay, queries, near, keep, gains)
     return call(
         finish_other, [smem] + [vmem] * 6, hbm, pltpu.HBM((T, heads * W), BF),
         [pltpu.VMEM((T, HALF * W), BF), pltpu.SemaphoreType.DMA((HALF // PART + 1,))], FINISH,
         cost_estimate=cost(1 << 27, 5 * MB),
-    )(which, started, log_decay, queries, inner, taken, gains)
+    )(which, started, log_decay, queries, far, taken, gains)
 
 
 def solution(mesh):

time: 57 us -> 56.1 us (0.984)
  Pallas kernels: 19.1 us -> 18.3 us
    pallas_call x3, Pallas kernels: 3.11 us -> 2.03 us  [the longest x1 1.6 us: on_device(): call(finish_own, [smem] + [vmem] * 5, vmem, struct((T, HALF * W), BF), li...]
  transfers between devices with their start and end apart: 3 -> 3, of which waited for: 1 -> 1; matrix products, arithmetic and copies ran while one was open for 0% -> 0% of each run, Pallas kernels for 23% -> 22%
where the time goes in v5:
time: 56.1 us; the launch traced here: 55.7 us
  Pallas kernels  18.3 us (33%)
  blocking collectives  15.8 us (28%)
  starting transfers between devices  15.7 us (28%)
  waiting for transfers between devices  5.7 us (10%)
    all_to_all x1, blocking collectives, on_device(): lax.all_to_all(before, CHIPS, split_axis=0, concat_axis=0, tiled=True)  15.8 us
    all_to_all x1, starting transfers between devices, on_device(): lax.all_to_all(chunks, CHIPS, split_axis=0, concat_axis=0, tiled=True)  11.2 us
    pallas_call x1, Pallas kernels, within_blocks(): pl.pallas_call(within, grid_spec=pltpu.PrefetchScalarGridSpec(num_scalar_...  8.48 us
    all_to_all x1, waiting for transfers between devices, on_device(): lax.all_to_all(chunks, CHIPS, split_axis=0, concat_axis=0, tiled=True)  5.69 us
    ppermute x1, starting transfers between devices, on_device(): taken = swap(give)  3 us
    pallas_call x1, Pallas kernels, on_device(): call(finish_other, [smem] + [vmem] * 6, hbm, pltpu.HBM((T, heads * W), BF...  2.43 us
    pallas_call x1, Pallas kernels, on_device(): call(own_states, [smem, hbm, hbm, hbm], [vmem, vmem], [struct((HALF, W, W...  2.18 us
    pallas_call x1, Pallas kernels, on_device(): call(send_states, [smem, hbm, hbm, hbm], vmem, struct((HALF * W + SPLIT,...  2.17 us
  transfers between devices with their start and end apart: 3, of which 1 were waited for; matrix products, arithmetic and copies ran while one was open for 0% of the time, Pallas kernels for 22%

profile of v5, /device:TPU:1, one launch (start us, length us, event | category | flops | bytes accessed | tf_op | source)
XLA Modules:
  0.0 55.7 jit_solution(15268179421456244751)
XLA Ops:
  0.0 2.2 %shard_map.56 = bf16[2096,128]{1,0:T(8,128)(2,1)S(1)} custom-call(s32[1]{0:T(128)} %bitcast.core_ref, bf16[256,4096]{1,0:T(8,128)(2,1)} %k_ref.5, bf16[256,4096]{1,0:T(8,128)(2,1)} %v_ref.5, f32[32,256]{1,0:T(8,128)} %ld_ref.9), custom_call_target="tpu_custom_call" | custom-call | flops 134217728 | bytes 3145728 | tf_op jit(solution)/shard_map/pallas_call | solution.py:301
  2.2 1.5 %collective-permute-start = (bf16[2096,128]{1,0:T(8,128)(2,1)S(1)}, bf16[2096,128]{1,0:T(8,128)(2,1)S(1)}, u32[]{:S(2)}, u32[]{:S(2)}) collective-permute-start(bf16[2096,128]{1,0:T(8,128)(2,1)S(1)} %shard_map.56), channel_id=1, source_target_pairs={{0,1},{1,0},{2,3},{3,2},{4,5},{5,4},{6,7},{7,6},{8,9},{9,8},{10,11... | collective-permute-start | bytes 1609736 | tf_op jit(solution)/shard_map/ppermute | solution.py:305
  3.7 2.2 %shard_map.55 = (f32[16,128,128]{2,1,0:T(8,128)S(1)}, f32[16,128]{1,0:T(8,128)S(1)}) custom-call(s32[1]{0:T(128)} %bitcast.core_ref, bf16[256,4096]{1,0:T(8,128)(2,1)} %k_ref.5, bf16[256,4096]{1,0:T(8,128)(2,1)} %v_ref.5, f32[32,256]{1,0:T(8,128)} %ld_ref.9), custom_call_target="tpu_custom_call" | custom-call | flops 134217728 | bytes 3145728 | tf_op jit(solution)/shard_map/pallas_call | solution.py:306
  5.9 0.0 collective-permute-done.recv_ref
  5.9 1.0 %shard_map.57 = (bf16[64,40,128]{2,1,0:T(8,128)(2,1)}, bf16[16,128,128]{2,1,0:T(8,128)(2,1)S(1)}, f32[16,128]{1,0:T(8,128)S(1)}) custom-call(s32[1]{0:T(128)} %bitcast.core_ref, f32[16,128,128]{2,1,0:T(8,128)S(1)} %get-tuple-element.19.own_ref, f32[16,128]{1,0:T(8,128)S(1)} %get-tuple-element.20.decay_ref, bf16[2096,128]{1,0:T(8,128)(2,1)S(1)} %collective-permute-done.recv_ref), custom_call_target="tpu_custom_call" | custom-call | tf_op jit(solution)/shard_map/pallas_call | solution.py:311
  6.9 11.2 %all-to-all-start = ((bf16[64,40,128]{2,1,0:T(8,128)(2,1)}), bf16[64,40,128]{2,1,0:T(8,128)(2,1)S(1)}, u32[]{:S(2)}, u32[]{:S(2)}) async-start(bf16[64,40,128]{2,1,0:T(8,128)(2,1)} %get-tuple-element.22), calls=%async_computation | async-start | bytes 1310720 | tf_op jit(solution)/shard_map/all_to_all | solution.py:316
  18.2 8.5 %shard_map.58 = (f32[256,2048]{1,0:T(8,128)}, f32[256,2048]{1,0:T(8,128)}) custom-call(s32[1]{0:T(128)} %bitcast.core_ref, f32[32,256]{1,0:T(8,128)} %ld_ref.9, bf16[256,4096]{1,0:T(8,128)(2,1)} %q_ref.4, bf16[256,4096]{1,0:T(8,128)(2,1)} %k_ref.5, bf16[256,4096]{1,0:T(8,128)(2,1)} %v_ref.5), custom_call_target="tpu_custom_call" | custom-call | flops 2147483648 | bytes 10485760 | tf_op jit(solution)/shard_map/pallas_call | solution.py:264
  26.6 0.0 copy-start
  26.6 5.7 %all-to-all-done.in_ref = bf16[64,40,128]{2,1,0:T(8,128)(2,1)S(1)} async-done(((bf16[64,40,128]{2,1,0:T(8,128)(2,1)}), bf16[64,40,128]{2,1,0:T(8,128)(2,1)S(1)}, u32[]{:S(2)}, u32[]{:S(2)}) %all-to-all-start) | async-done | bytes 655392 | tf_op jit(solution)/shard_map/all_to_all | solution.py:316
  32.3 0.2 shard_map.59
  32.5 0.0 copy-start.1
  32.5 0.0 copy-start.3
  32.5 0.0 copy-start.4
  32.5 15.8 %all_to_all.10.chip_ref = bf16[64,32,128]{2,1,0:T(8,128)(2,1)S(1)} all-to-all(bf16[64,32,128]{2,1,0:T(8,128)(2,1)S(1)} %shard_map.59), channel_id=1, replica_groups=mesh['z'=4,'y'=4,'x'=4,'c'=2] {'z','y','x'}, dimensions={0} | all-to-all | bytes 1048576 | tf_op jit(solution)/shard_map/all_to_all | solution.py:320
  48.3 0.0 copy-done
  48.4 0.3 shard_map.60
  48.6 3.0 %collective-permute-start.1 = (bf16[16,128,128]{2,1,0:T(8,128)(2,1)S(1)}, bf16[16,128,128]{2,1,0:T(8,128)(2,1)S(1)}, u32[]{:S(2)}, u32[]{:S(2)}) collective-permute-start(bf16[16,128,128]{2,1,0:T(8,128)(2,1)S(1)} %get-tuple-element.32), channel_id=1, source_target_pairs={{0,1},{1,0},{2,3},{3,2},{4,5},{5,4},{6,7},{7,6},{8,9},{9,8},{10,11... | collective-permute-start | bytes 1572872 | tf_op jit(solution)/shard_map/ppermute | solution.py:325
  51.6 0.0 copy-done.1
  51.6 0.0 copy-done.3
  51.6 0.0 copy-done.4
  51.6 0.0 copy-start.2
  51.6 1.6 %shard_map.61.own_ref = bf16[256,2048]{1,0:T(8,128)(2,1)S(1)} custom-call(s32[1]{0:T(128)} %bitcast.core_ref, f32[32,256]{1,0:T(8,128)S(1)} %copy-done.3, bf16[256,4096]{1,0:T(8,128)(2,1)S(1)} %copy-done.1, f32[256,2048]{1,0:T(8,128)S(1)} %copy-done, bf16[16,128,128]{2,1,0:T(8,128)(2,1)S(1)} %get-tuple-element.30.carried_ref, f32[1,4096]{1,0:T(1,128)S(1)} %bitcast.2), custom_call_target="tpu_custom_call" | custom-call | flops 134217728 | bytes 5242880 | tf_op jit(solution)/shard_map/pallas_call | solution.py:327
  53.2 0.0 collective-permute-done.1.carried_ref
  53.2 0.0 copy-done.2
  53.3 2.4 %shard_map.62 = bf16[256,4096]{1,0:T(8,128)(2,1)} custom-call(s32[1]{0:T(128)} %bitcast.core_ref, bf16[256,2048]{1,0:T(8,128)(2,1)S(1)} %shard_map.61.own_ref, f32[32,256]{1,0:T(8,128)S(1)} %copy-done.3, bf16[256,4096]{1,0:T(8,128)(2,1)S(1)} %copy-done.1, f32[256,2048]{1,0:T(8,128)S(1)} %copy-done.2, ...), custom_call_target="tpu_custom_call" | custom-call | flops 134217728 | bytes 5242880 | tf_op jit(solution)/shard_map/pallas_call | solution.py:331
Async XLA Ops:
  2.2 3.7 %collective-permute-start = (bf16[2096,128]{1,0:T(8,128)(2,1)S(1)}, bf16[2096,128]{1,0:T(8,128)(2,1)S(1)}, u32[]{:S(2)}, u32[]{:S(2)}) collective-permute-start(bf16[2096,128]{1,0:T(8,128)(2,1)S(1)} %shard_map.56), channel_id=1, source_target_pairs={{0,1},{1,0},{2,3},{3,2},{4,5},{5,4},{6,7},{7,6},{8,9},{9,8},{10,11... | collective-permute-start | bytes 1609736 | tf_op jit(solution)/shard_map/ppermute | solution.py:305
  6.9 25.4 %all-to-all-start = ((bf16[64,40,128]{2,1,0:T(8,128)(2,1)}), bf16[64,40,128]{2,1,0:T(8,128)(2,1)S(1)}, u32[]{:S(2)}, u32[]{:S(2)}) async-start(bf16[64,40,128]{2,1,0:T(8,128)(2,1)} %get-tuple-element.22), calls=%async_computation | async-start | bytes 1310720 | tf_op jit(solution)/shard_map/all_to_all | solution.py:316
  26.6 21.7 %copy-start = (f32[256,2048]{1,0:T(8,128)S(1)}, f32[256,2048]{1,0:T(8,128)}, u32[]{:S(2)}) copy-start(f32[256,2048]{1,0:T(8,128)} %get-tuple-element.26.near_ref.inner_ref) | copy-start | bytes 6291460
  32.5 19.1 %copy-start.1 = (bf16[256,4096]{1,0:T(8,128)(2,1)S(1)}, bf16[256,4096]{1,0:T(8,128)(2,1)}, u32[]{:S(2)}) copy-start(bf16[256,4096]{1,0:T(8,128)(2,1)} %q_ref.4) | copy-start | bytes 6291460
  32.5 19.1 %copy-start.3 = (f32[32,256]{1,0:T(8,128)S(1)}, f32[32,256]{1,0:T(8,128)}, u32[]{:S(2)}) copy-start(f32[32,256]{1,0:T(8,128)} %ld_ref.9) | copy-start | bytes 98308
  32.5 19.1 %copy-start.4 = (f32[4096]{0:T(1024)S(1)}, f32[4096]{0:T(1024)}, u32[]{:S(2)}) copy-start(f32[4096]{0:T(1024)} %param.9) | copy-start | bytes 49156
  48.6 4.6 %collective-permute-start.1 = (bf16[16,128,128]{2,1,0:T(8,128)(2,1)S(1)}, bf16[16,128,128]{2,1,0:T(8,128)(2,1)S(1)}, u32[]{:S(2)}, u32[]{:S(2)}) collective-permute-start(bf16[16,128,128]{2,1,0:T(8,128)(2,1)S(1)} %get-tuple-element.32), channel_id=1, source_target_pairs={{0,1},{1,0},{2,3},{3,2},{4,5},{5,4},{6,7},{7,6},{8,9},{9,8},{10,11... | collective-permute-start | bytes 1572872 | tf_op jit(solution)/shard_map/ppermute | solution.py:325
  51.6 1.6 %copy-start.2 = (f32[256,2048]{1,0:T(8,128)S(1)}, f32[256,2048]{1,0:T(8,128)}, u32[]{:S(2)}) copy-start(f32[256,2048]{1,0:T(8,128)} %get-tuple-element.31.inner_ref) | copy-start | bytes 6291460

commit v6 on v5

--- a/solution.py
+++ b/solution.py
@@ -19,6 +19,7 @@
 SPLIT = 48
 ROWS = 40
 AHEAD = 1
+READY = 4
 PART = 4
 MB = 1 << 20
 LIMIT = 12
@@ -50,7 +51,7 @@
     rows = pl.ds(pl.multiple_of(half * HALF, HALF), HALF)
     views = [r.at[:, columns] for r in refs[:-1]] + [refs[-1].at[rows, :]]
     copies = [pltpu.make_async_copy(v, b, sem.at[n]) for n, (v, b) in enumerate(zip(views, bufs))]
-    for c in reversed(copies):
+    for c in (copies[-1], *copies[:-1]):
         c.start()
     return copies
 
@@ -67,11 +68,11 @@
         kt = kbuf[:, j * W : (j + 1) * W].T
         return (kt.astype(F32) * factor[j : j + 1, :]).astype(BF)
 
-    ready = [decayed(0), decayed(1)]
+    ready = [decayed(j) for j in range(READY)]
     v_in.wait()
     for j in range(HALF):
-        if j + 2 < HALF:
-            ready.append(decayed(j + 2))
+        if j + READY < HALF:
+            ready.append(decayed(j + READY))
         put(j, dot(ready[j], vbuf[:, j * W : (j + 1) * W]))
     return jnp.broadcast_to(jnp.exp(total), (HALF, W))
 

time: 56.1 us -> 55.8 us (level)
  no operation moved by 1% of the time
where the time goes in v6:
time: 55.8 us; the launch traced here: 55.4 us
  Pallas kernels  18.1 us (32%)
  blocking collectives  15.8 us (28%)
  starting transfers between devices  15.7 us (28%)
  waiting for transfers between devices  5.7 us (10%)
    all_to_all x1, blocking collectives, on_device(): lax.all_to_all(before, CHIPS, split_axis=0, concat_axis=0, tiled=True)  15.8 us
    all_to_all x1, starting transfers between devices, on_device(): lax.all_to_all(chunks, CHIPS, split_axis=0, concat_axis=0, tiled=True)  11.2 us
    pallas_call x1, Pallas kernels, within_blocks(): pl.pallas_call(within, grid_spec=pltpu.PrefetchScalarGridSpec(num_scalar_...  8.49 us
    all_to_all x1, waiting for transfers between devices, on_device(): lax.all_to_all(chunks, CHIPS, split_axis=0, concat_axis=0, tiled=True)  5.69 us
    ppermute x1, starting transfers between devices, on_device(): taken = swap(give)  3 us
    pallas_call x1, Pallas kernels, on_device(): call(finish_other, [smem] + [vmem] * 6, hbm, pltpu.HBM((T, heads * W), BF...  2.43 us
    pallas_call x1, Pallas kernels, on_device(): call(own_states, [smem, hbm, hbm, hbm], [vmem, vmem], [struct((HALF, W, W...  2.05 us
    pallas_call x1, Pallas kernels, on_device(): call(send_states, [smem, hbm, hbm, hbm], vmem, struct((HALF * W + SPLIT,...  2.04 us
  transfers between devices with their start and end apart: 3, of which 1 were waited for; matrix products, arithmetic and copies ran while one was open for 0% of the time, Pallas kernels for 22%

profile of v6, /device:TPU:1, one launch (start us, length us, event | category | flops | bytes accessed | tf_op | source)
XLA Modules:
  0.0 55.4 jit_solution(12607175530814984734)
XLA Ops:
  0.0 2.0 %shard_map.56 = bf16[2096,128]{1,0:T(8,128)(2,1)S(1)} custom-call(s32[1]{0:T(128)} %bitcast.core_ref, bf16[256,4096]{1,0:T(8,128)(2,1)} %k_ref.5, bf16[256,4096]{1,0:T(8,128)(2,1)} %v_ref.5, f32[32,256]{1,0:T(8,128)} %ld_ref.9), custom_call_target="tpu_custom_call" | custom-call | flops 134217728 | bytes 3145728 | tf_op jit(solution)/shard_map/pallas_call | solution.py:302
  2.0 1.5 %collective-permute-start = (bf16[2096,128]{1,0:T(8,128)(2,1)S(1)}, bf16[2096,128]{1,0:T(8,128)(2,1)S(1)}, u32[]{:S(2)}, u32[]{:S(2)}) collective-permute-start(bf16[2096,128]{1,0:T(8,128)(2,1)S(1)} %shard_map.56), channel_id=1, source_target_pairs={{0,1},{1,0},{2,3},{3,2},{4,5},{5,4},{6,7},{7,6},{8,9},{9,8},{10,11... | collective-permute-start | bytes 1609736 | tf_op jit(solution)/shard_map/ppermute | solution.py:306
  3.5 2.1 %shard_map.55 = (f32[16,128,128]{2,1,0:T(8,128)S(1)}, f32[16,128]{1,0:T(8,128)S(1)}) custom-call(s32[1]{0:T(128)} %bitcast.core_ref, bf16[256,4096]{1,0:T(8,128)(2,1)} %k_ref.5, bf16[256,4096]{1,0:T(8,128)(2,1)} %v_ref.5, f32[32,256]{1,0:T(8,128)} %ld_ref.9), custom_call_target="tpu_custom_call" | custom-call | flops 134217728 | bytes 3145728 | tf_op jit(solution)/shard_map/pallas_call | solution.py:307
  5.6 0.0 collective-permute-done.recv_ref
  5.6 1.0 %shard_map.57 = (bf16[64,40,128]{2,1,0:T(8,128)(2,1)}, bf16[16,128,128]{2,1,0:T(8,128)(2,1)S(1)}, f32[16,128]{1,0:T(8,128)S(1)}) custom-call(s32[1]{0:T(128)} %bitcast.core_ref, f32[16,128,128]{2,1,0:T(8,128)S(1)} %get-tuple-element.19.own_ref, f32[16,128]{1,0:T(8,128)S(1)} %get-tuple-element.20.decay_ref, bf16[2096,128]{1,0:T(8,128)(2,1)S(1)} %collective-permute-done.recv_ref), custom_call_target="tpu_custom_call" | custom-call | tf_op jit(solution)/shard_map/pallas_call | solution.py:312
  6.7 11.2 %all-to-all-start = ((bf16[64,40,128]{2,1,0:T(8,128)(2,1)}), bf16[64,40,128]{2,1,0:T(8,128)(2,1)S(1)}, u32[]{:S(2)}, u32[]{:S(2)}) async-start(bf16[64,40,128]{2,1,0:T(8,128)(2,1)} %get-tuple-element.22), calls=%async_computation | async-start | bytes 1310720 | tf_op jit(solution)/shard_map/all_to_all | solution.py:317
  17.9 8.5 %shard_map.58 = (f32[256,2048]{1,0:T(8,128)}, f32[256,2048]{1,0:T(8,128)}) custom-call(s32[1]{0:T(128)} %bitcast.core_ref, f32[32,256]{1,0:T(8,128)} %ld_ref.9, bf16[256,4096]{1,0:T(8,128)(2,1)} %q_ref.4, bf16[256,4096]{1,0:T(8,128)(2,1)} %k_ref.5, bf16[256,4096]{1,0:T(8,128)(2,1)} %v_ref.5), custom_call_target="tpu_custom_call" | custom-call | flops 2147483648 | bytes 10485760 | tf_op jit(solution)/shard_map/pallas_call | solution.py:265
  26.4 0.0 copy-start
  26.4 5.7 %all-to-all-done.in_ref = bf16[64,40,128]{2,1,0:T(8,128)(2,1)S(1)} async-done(((bf16[64,40,128]{2,1,0:T(8,128)(2,1)}), bf16[64,40,128]{2,1,0:T(8,128)(2,1)S(1)}, u32[]{:S(2)}, u32[]{:S(2)}) %all-to-all-start) | async-done | bytes 655392 | tf_op jit(solution)/shard_map/all_to_all | solution.py:317
  32.1 0.2 shard_map.59
  32.2 0.0 copy-start.1
  32.3 0.0 copy-start.3
  32.3 0.0 copy-start.4
  32.3 15.8 %all_to_all.10.chip_ref = bf16[64,32,128]{2,1,0:T(8,128)(2,1)S(1)} all-to-all(bf16[64,32,128]{2,1,0:T(8,128)(2,1)S(1)} %shard_map.59), channel_id=1, replica_groups=mesh['z'=4,'y'=4,'x'=4,'c'=2] {'z','y','x'}, dimensions={0} | all-to-all | bytes 1048576 | tf_op jit(solution)/shard_map/all_to_all | solution.py:321
  48.1 0.0 copy-done
  48.1 0.3 shard_map.60
  48.3 3.0 %collective-permute-start.1 = (bf16[16,128,128]{2,1,0:T(8,128)(2,1)S(1)}, bf16[16,128,128]{2,1,0:T(8,128)(2,1)S(1)}, u32[]{:S(2)}, u32[]{:S(2)}) collective-permute-start(bf16[16,128,128]{2,1,0:T(8,128)(2,1)S(1)} %get-tuple-element.32), channel_id=1, source_target_pairs={{0,1},{1,0},{2,3},{3,2},{4,5},{5,4},{6,7},{7,6},{8,9},{9,8},{10,11... | collective-permute-start | bytes 1572872 | tf_op jit(solution)/shard_map/ppermute | solution.py:326
  51.4 0.0 copy-done.1
  51.4 0.0 copy-done.3
  51.4 0.0 copy-done.4
  51.4 0.0 copy-start.2
  51.4 1.6 %shard_map.61.own_ref = bf16[256,2048]{1,0:T(8,128)(2,1)S(1)} custom-call(s32[1]{0:T(128)} %bitcast.core_ref, f32[32,256]{1,0:T(8,128)S(1)} %copy-done.3, bf16[256,4096]{1,0:T(8,128)(2,1)S(1)} %copy-done.1, f32[256,2048]{1,0:T(8,128)S(1)} %copy-done, bf16[16,128,128]{2,1,0:T(8,128)(2,1)S(1)} %get-tuple-element.30.carried_ref, f32[1,4096]{1,0:T(1,128)S(1)} %bitcast.2), custom_call_target="tpu_custom_call" | custom-call | flops 134217728 | bytes 5242880 | tf_op jit(solution)/shard_map/pallas_call | solution.py:328
  53.0 0.0 collective-permute-done.1.carried_ref
  53.0 0.0 copy-done.2
  53.0 2.4 %shard_map.62 = bf16[256,4096]{1,0:T(8,128)(2,1)} custom-call(s32[1]{0:T(128)} %bitcast.core_ref, bf16[256,2048]{1,0:T(8,128)(2,1)S(1)} %shard_map.61.own_ref, f32[32,256]{1,0:T(8,128)S(1)} %copy-done.3, bf16[256,4096]{1,0:T(8,128)(2,1)S(1)} %copy-done.1, f32[256,2048]{1,0:T(8,128)S(1)} %copy-done.2, ...), custom_call_target="tpu_custom_call" | custom-call | flops 134217728 | bytes 5242880 | tf_op jit(solution)/shard_map/pallas_call | solution.py:332
Async XLA Ops:
  2.0 3.6 %collective-permute-start = (bf16[2096,128]{1,0:T(8,128)(2,1)S(1)}, bf16[2096,128]{1,0:T(8,128)(2,1)S(1)}, u32[]{:S(2)}, u32[]{:S(2)}) collective-permute-start(bf16[2096,128]{1,0:T(8,128)(2,1)S(1)} %shard_map.56), channel_id=1, source_target_pairs={{0,1},{1,0},{2,3},{3,2},{4,5},{5,4},{6,7},{7,6},{8,9},{9,8},{10,11... | collective-permute-start | bytes 1609736 | tf_op jit(solution)/shard_map/ppermute | solution.py:306
  6.7 25.4 %all-to-all-start = ((bf16[64,40,128]{2,1,0:T(8,128)(2,1)}), bf16[64,40,128]{2,1,0:T(8,128)(2,1)S(1)}, u32[]{:S(2)}, u32[]{:S(2)}) async-start(bf16[64,40,128]{2,1,0:T(8,128)(2,1)} %get-tuple-element.22), calls=%async_computation | async-start | bytes 1310720 | tf_op jit(solution)/shard_map/all_to_all | solution.py:317
  26.4 21.7 %copy-start = (f32[256,2048]{1,0:T(8,128)S(1)}, f32[256,2048]{1,0:T(8,128)}, u32[]{:S(2)}) copy-start(f32[256,2048]{1,0:T(8,128)} %get-tuple-element.26.near_ref.inner_ref) | copy-start | bytes 6291460
  32.2 19.1 %copy-start.1 = (bf16[256,4096]{1,0:T(8,128)(2,1)S(1)}, bf16[256,4096]{1,0:T(8,128)(2,1)}, u32[]{:S(2)}) copy-start(bf16[256,4096]{1,0:T(8,128)(2,1)} %q_ref.4) | copy-start | bytes 6291460
  32.3 19.1 %copy-start.3 = (f32[32,256]{1,0:T(8,128)S(1)}, f32[32,256]{1,0:T(8,128)}, u32[]{:S(2)}) copy-start(f32[32,256]{1,0:T(8,128)} %ld_ref.9) | copy-start | bytes 98308
  32.3 19.1 %copy-start.4 = (f32[4096]{0:T(1024)S(1)}, f32[4096]{0:T(1024)}, u32[]{:S(2)}) copy-start(f32[4096]{0:T(1024)} %param.9) | copy-start | bytes 49156
  48.3 4.6 %collective-permute-start.1 = (bf16[16,128,128]{2,1,0:T(8,128)(2,1)S(1)}, bf16[16,128,128]{2,1,0:T(8,128)(2,1)S(1)}, u32[]{:S(2)}, u32[]{:S(2)}) collective-permute-start(bf16[16,128,128]{2,1,0:T(8,128)(2,1)S(1)} %get-tuple-element.32), channel_id=1, source_target_pairs={{0,1},{1,0},{2,3},{3,2},{4,5},{5,4},{6,7},{7,6},{8,9},{9,8},{10,11... | collective-permute-start | bytes 1572872 | tf_op jit(solution)/shard_map/ppermute | solution.py:326
  51.4 1.6 %copy-start.2 = (f32[256,2048]{1,0:T(8,128)S(1)}, f32[256,2048]{1,0:T(8,128)}, u32[]{:S(2)}) copy-start(f32[256,2048]{1,0:T(8,128)} %get-tuple-element.31.inner_ref) | copy-start | bytes 6291460

commit v7 on v6

--- a/solution.py
+++ b/solution.py
@@ -130,16 +130,16 @@
         carry = decay * carry + x[:32]
 
 
-def spread_back(core_ref, near_ref, chip_ref, first_ref, first_decay_ref, keep_ref, send_ref):
-    earlier = core_ref[0] == 0
+def before_block(chip_ref, first_ref, decay, wants_first, h):
+    first = chip_ref[4 * h : 4 * h + 4].reshape(W, W).astype(F32)
+    second = decay[h : h + 1] * first + first_ref[h].astype(F32)
+    return jnp.where(wants_first, first, second).astype(BF)
+
+
+def spread_back(core_ref, near_ref, chip_ref, first_ref, first_decay_ref, send_ref):
     decay = first_decay_ref[...]
     for h in range(HALF):
-        for r in range(4):
-            rows = slice(r * 32, (r + 1) * 32)
-            first = chip_ref[4 * h + r].astype(F32)
-            second = decay[h : h + 1] * first + first_ref[h, rows, :].astype(F32)
-            keep_ref[h, rows, :] = jnp.where(earlier, first, second).astype(BF)
-            send_ref[h, rows, :] = jnp.where(earlier, second, first).astype(BF)
+        send_ref[h] = before_block(chip_ref, first_ref, decay, core_ref[0] != 0, h)
 
 
 def within(core_ref, ld_ref, q_ref, k_ref, v_ref, near_ref, far_ref):
@@ -193,7 +193,7 @@
     total(HB - 1, *waiting)
 
 
-def finish_half(half, ld_ref, q_ref, inner_ref, carried_ref, gain_ref, put):
+def finish_half(half, ld_ref, q_ref, inner_ref, carried, gain_ref, put):
     grown = jnp.exp(running(ld_ref[pl.ds(pl.multiple_of(half * HALF, HALF), HALF), :])).T
     ones = jnp.full((W, W), 1.0 / W, BF)
 
@@ -201,7 +201,7 @@
         return pl.ds(pl.multiple_of(half * HALF * W + j * W, W), W)
 
     def readout(j):
-        return dot(q_ref[:, columns(j)], carried_ref[j])
+        return dot(q_ref[:, columns(j)], carried(j))
 
     ready = [readout(j) for j in range(AHEAD)]
     for j in range(HALF):
@@ -213,11 +213,16 @@
         put(j, (numer * lax.rsqrt(mean + 1e-6) * gain_ref[:, columns(j)]).astype(BF))
 
 
-def finish_own(core_ref, ld_ref, q_ref, inner_ref, carried_ref, gain_ref, out_ref):
+def finish_own(core_ref, ld_ref, q_ref, inner_ref, chip_ref, first_ref, first_decay_ref, gain_ref, out_ref):
+    decay = first_decay_ref[...]
+
+    def carried(j):
+        return before_block(chip_ref, first_ref, decay, core_ref[0] == 0, j)
+
     def put(j, value):
         out_ref[:, j * W : (j + 1) * W] = value
 
-    finish_half(core_ref[0], ld_ref, q_ref, inner_ref, carried_ref, gain_ref, put)
+    finish_half(core_ref[0], ld_ref, q_ref, inner_ref, carried, gain_ref, put)
 
 
 def finish_other(core_ref, own_ref, ld_ref, q_ref, inner_ref, carried_ref, gain_ref, out_ref, buf, sem):
@@ -235,7 +240,7 @@
             copy.start()
             copies.append(copy)
 
-    finish_half(half, ld_ref, q_ref, inner_ref, carried_ref, gain_ref, put)
+    finish_half(half, ld_ref, q_ref, inner_ref, lambda j: carried_ref[j], gain_ref, put)
     for copy in copies:
         copy.wait()
 
@@ -319,16 +324,16 @@
     owned, near, far = lax.optimization_barrier((owned, near, far))
     before = call(scan_chips, [vmem], vmem, struct((chips, 32, W), BF), cost_estimate=cost(1 << 10, 1 << 10))(owned)
     back = lax.all_to_all(before, CHIPS, split_axis=0, concat_axis=0, tiled=True)
-    keep, give = call(
-        spread_back, [smem, vmem, vmem, vmem, vmem], [vmem] * 2, [struct((HALF, W, W), BF)] * 2,
+    give = call(
+        spread_back, [smem, vmem, vmem, vmem, vmem], vmem, struct((HALF, W, W), BF),
         cost_estimate=cost(1 << 10, 1 << 10),
     )(which, near, back, first, first_decay)
     taken = swap(give)
     gains = gain.reshape(1, heads * W)
     started = call(
-        finish_own, [smem] + [vmem] * 5, vmem, struct((T, HALF * W), BF), limit=FINISH,
+        finish_own, [smem] + [vmem] * 7, vmem, struct((T, HALF * W), BF), limit=FINISH,
         cost_estimate=cost(1 << 27, 5 * MB),
-    )(which, log_decay, queries, near, keep, gains)
+    )(which, log_decay, queries, near, back, first, first_decay, gains)
     return call(
         finish_other, [smem] + [vmem] * 6, hbm, pltpu.HBM((T, heads * W), BF),
         [pltpu.VMEM((T, HALF * W), BF), pltpu.SemaphoreType.DMA((HALF // PART + 1,))], FINISH,

time: 55.8 us -> 55.6 us (level)
  no operation moved by 1% of the time
where the time goes in v7:
time: 55.6 us; the launch traced here: 55.2 us
  Pallas kernels  18 us (32%)
  starting transfers between devices  15.7 us (28%)
  blocking collectives  15.7 us (28%)
  waiting for transfers between devices  5.7 us (10%)
    all_to_all x1, blocking collectives, on_device(): lax.all_to_all(before, CHIPS, split_axis=0, concat_axis=0, tiled=True)  15.7 us
    all_to_all x1, starting transfers between devices, on_device(): lax.all_to_all(chunks, CHIPS, split_axis=0, concat_axis=0, tiled=True)  11.2 us
    pallas_call x1, Pallas kernels, within_blocks(): pl.pallas_call(within, grid_spec=pltpu.PrefetchScalarGridSpec(num_scalar_...  8.48 us
    all_to_all x1, waiting for transfers between devices, on_device(): lax.all_to_all(chunks, CHIPS, split_axis=0, concat_axis=0, tiled=True)  5.7 us
    ppermute x1, starting transfers between devices, on_device(): taken = swap(give)  3 us
    pallas_call x1, Pallas kernels, on_device(): call(finish_other, [smem] + [vmem] * 6, hbm, pltpu.HBM((T, heads * W), BF...  2.42 us
    pallas_call x1, Pallas kernels, on_device(): call(own_states, [smem, hbm, hbm, hbm], [vmem, vmem], [struct((HALF, W, W...  2.05 us
    pallas_call x1, Pallas kernels, on_device(): call(send_states, [smem, hbm, hbm, hbm], vmem, struct((HALF * W + SPLIT,...  2.04 us
  transfers between devices with their start and end apart: 3, of which 1 were waited for; matrix products, arithmetic and copies ran while one was open for 0% of the time, Pallas kernels for 22%

profile of v7, /device:TPU:1, one launch (start us, length us, event | category | flops | bytes accessed | tf_op | source)
XLA Modules:
  0.0 55.2 jit_solution(7441712901295425076)
XLA Ops:
  0.0 2.0 %shard_map.56 = bf16[2096,128]{1,0:T(8,128)(2,1)S(1)} custom-call(s32[1]{0:T(128)} %bitcast.core_ref, bf16[256,4096]{1,0:T(8,128)(2,1)} %k_ref.5, bf16[256,4096]{1,0:T(8,128)(2,1)} %v_ref.5, f32[32,256]{1,0:T(8,128)} %ld_ref.9), custom_call_target="tpu_custom_call" | custom-call | flops 134217728 | bytes 3145728 | tf_op jit(solution)/shard_map/pallas_call | solution.py:307
  2.0 1.5 %collective-permute-start = (bf16[2096,128]{1,0:T(8,128)(2,1)S(1)}, bf16[2096,128]{1,0:T(8,128)(2,1)S(1)}, u32[]{:S(2)}, u32[]{:S(2)}) collective-permute-start(bf16[2096,128]{1,0:T(8,128)(2,1)S(1)} %shard_map.56), channel_id=1, source_target_pairs={{0,1},{1,0},{2,3},{3,2},{4,5},{5,4},{6,7},{7,6},{8,9},{9,8},{10,11... | collective-permute-start | bytes 1609736 | tf_op jit(solution)/shard_map/ppermute | solution.py:311
  3.5 2.1 %shard_map.55 = (f32[16,128,128]{2,1,0:T(8,128)S(1)}, f32[16,128]{1,0:T(8,128)S(1)}) custom-call(s32[1]{0:T(128)} %bitcast.core_ref, bf16[256,4096]{1,0:T(8,128)(2,1)} %k_ref.5, bf16[256,4096]{1,0:T(8,128)(2,1)} %v_ref.5, f32[32,256]{1,0:T(8,128)} %ld_ref.9), custom_call_target="tpu_custom_call" | custom-call | flops 134217728 | bytes 3145728 | tf_op jit(solution)/shard_map/pallas_call | solution.py:312
  5.6 0.0 collective-permute-done.recv_ref
  5.6 1.1 %shard_map.57 = (bf16[64,40,128]{2,1,0:T(8,128)(2,1)}, bf16[16,128,128]{2,1,0:T(8,128)(2,1)S(1)}, f32[16,128]{1,0:T(8,128)S(1)}) custom-call(s32[1]{0:T(128)} %bitcast.core_ref, f32[16,128,128]{2,1,0:T(8,128)S(1)} %get-tuple-element.17.own_ref, f32[16,128]{1,0:T(8,128)S(1)} %get-tuple-element.18.decay_ref, bf16[2096,128]{1,0:T(8,128)(2,1)S(1)} %collective-permute-done.recv_ref), custom_call_target="tpu_custom_call" | custom-call | tf_op jit(solution)/shard_map/pallas_call | solution.py:317
  6.7 11.2 %all-to-all-start = ((bf16[64,40,128]{2,1,0:T(8,128)(2,1)}), bf16[64,40,128]{2,1,0:T(8,128)(2,1)S(1)}, u32[]{:S(2)}, u32[]{:S(2)}) async-start(bf16[64,40,128]{2,1,0:T(8,128)(2,1)} %get-tuple-element.20), calls=%async_computation | async-start | bytes 1310720 | tf_op jit(solution)/shard_map/all_to_all | solution.py:322
  17.9 8.5 %shard_map.58 = (f32[256,2048]{1,0:T(8,128)}, f32[256,2048]{1,0:T(8,128)}) custom-call(s32[1]{0:T(128)} %bitcast.core_ref, f32[32,256]{1,0:T(8,128)} %ld_ref.9, bf16[256,4096]{1,0:T(8,128)(2,1)} %q_ref.4, bf16[256,4096]{1,0:T(8,128)(2,1)} %k_ref.5, bf16[256,4096]{1,0:T(8,128)(2,1)} %v_ref.5), custom_call_target="tpu_custom_call" | custom-call | flops 2147483648 | bytes 10485760 | tf_op jit(solution)/shard_map/pallas_call | solution.py:270
  26.4 0.0 copy-start
  26.4 5.7 %all-to-all-done.in_ref = bf16[64,40,128]{2,1,0:T(8,128)(2,1)S(1)} async-done(((bf16[64,40,128]{2,1,0:T(8,128)(2,1)}), bf16[64,40,128]{2,1,0:T(8,128)(2,1)S(1)}, u32[]{:S(2)}, u32[]{:S(2)}) %all-to-all-start) | async-done | bytes 655392 | tf_op jit(solution)/shard_map/all_to_all | solution.py:322
  32.1 0.2 shard_map.59
  32.2 15.7 %all_to_all.10.chip_ref = bf16[64,32,128]{2,1,0:T(8,128)(2,1)S(1)} all-to-all(bf16[64,32,128]{2,1,0:T(8,128)(2,1)S(1)} %shard_map.59), channel_id=1, replica_groups=mesh['z'=4,'y'=4,'x'=4,'c'=2] {'z','y','x'}, dimensions={0} | all-to-all | bytes 1048576 | tf_op jit(solution)/shard_map/all_to_all | solution.py:326
  47.9 0.0 copy-start.1
  47.9 0.0 copy-start.3
  47.9 0.0 copy-start.4
  47.9 0.0 copy-done
  47.9 0.2 shard_map.61
  48.1 3.0 %collective-permute-start.1 = (bf16[16,128,128]{2,1,0:T(8,128)(2,1)S(1)}, bf16[16,128,128]{2,1,0:T(8,128)(2,1)S(1)}, u32[]{:S(2)}, u32[]{:S(2)}) collective-permute-start(bf16[16,128,128]{2,1,0:T(8,128)(2,1)S(1)} %shard_map.61), channel_id=1, source_target_pairs={{0,1},{1,0},{2,3},{3,2},{4,5},{5,4},{6,7},{7,6},{8,9},{9,8},{10,11... | collective-permute-start | bytes 1572872 | tf_op jit(solution)/shard_map/ppermute | solution.py:331
  51.1 0.0 copy-done.1
  51.1 0.0 copy-done.3
  51.1 0.0 copy-done.4
  51.1 0.0 copy-start.2
  51.1 1.6 %shard_map.60.own_ref = bf16[256,2048]{1,0:T(8,128)(2,1)S(1)} custom-call(s32[1]{0:T(128)} %bitcast.core_ref, f32[32,256]{1,0:T(8,128)S(1)} %copy-done.3, bf16[256,4096]{1,0:T(8,128)(2,1)S(1)} %copy-done.1, f32[256,2048]{1,0:T(8,128)S(1)} %copy-done, bf16[64,32,128]{2,1,0:T(8,128)(2,1)S(1)} %all_to_all.10.chip_ref, ...), custom_call_target="tpu_custom_call" | custom-call | flops 134217728 | bytes 5242880 | tf_op jit(solution)/shard_map/pallas_call | solution.py:333
  52.8 0.0 collective-permute-done.1.carried_ref
  52.8 0.0 copy-done.2
  52.8 2.4 %shard_map.62 = bf16[256,4096]{1,0:T(8,128)(2,1)} custom-call(s32[1]{0:T(128)} %bitcast.core_ref, bf16[256,2048]{1,0:T(8,128)(2,1)S(1)} %shard_map.60.own_ref, f32[32,256]{1,0:T(8,128)S(1)} %copy-done.3, bf16[256,4096]{1,0:T(8,128)(2,1)S(1)} %copy-done.1, f32[256,2048]{1,0:T(8,128)S(1)} %copy-done.2, ...), custom_call_target="tpu_custom_call" | custom-call | flops 134217728 | bytes 5242880 | tf_op jit(solution)/shard_map/pallas_call | solution.py:337
Async XLA Ops:
  2.0 3.6 %collective-permute-start = (bf16[2096,128]{1,0:T(8,128)(2,1)S(1)}, bf16[2096,128]{1,0:T(8,128)(2,1)S(1)}, u32[]{:S(2)}, u32[]{:S(2)}) collective-permute-start(bf16[2096,128]{1,0:T(8,128)(2,1)S(1)} %shard_map.56), channel_id=1, source_target_pairs={{0,1},{1,0},{2,3},{3,2},{4,5},{5,4},{6,7},{7,6},{8,9},{9,8},{10,11... | collective-permute-start | bytes 1609736 | tf_op jit(solution)/shard_map/ppermute | solution.py:311
  6.7 25.4 %all-to-all-start = ((bf16[64,40,128]{2,1,0:T(8,128)(2,1)}), bf16[64,40,128]{2,1,0:T(8,128)(2,1)S(1)}, u32[]{:S(2)}, u32[]{:S(2)}) async-start(bf16[64,40,128]{2,1,0:T(8,128)(2,1)} %get-tuple-element.20), calls=%async_computation | async-start | bytes 1310720 | tf_op jit(solution)/shard_map/all_to_all | solution.py:322
  26.4 21.6 %copy-start = (f32[256,2048]{1,0:T(8,128)S(1)}, f32[256,2048]{1,0:T(8,128)}, u32[]{:S(2)}) copy-start(f32[256,2048]{1,0:T(8,128)} %get-tuple-element.24.inner_ref.near_ref) | copy-start | bytes 6291460
  47.9 3.2 %copy-start.1 = (bf16[256,4096]{1,0:T(8,128)(2,1)S(1)}, bf16[256,4096]{1,0:T(8,128)(2,1)}, u32[]{:S(2)}) copy-start(bf16[256,4096]{1,0:T(8,128)(2,1)} %q_ref.4) | copy-start | bytes 6291460
  47.9 3.2 %copy-start.3 = (f32[32,256]{1,0:T(8,128)S(1)}, f32[32,256]{1,0:T(8,128)}, u32[]{:S(2)}) copy-start(f32[32,256]{1,0:T(8,128)} %ld_ref.9) | copy-start | bytes 98308
  47.9 3.2 %copy-start.4 = (f32[4096]{0:T(1024)S(1)}, f32[4096]{0:T(1024)}, u32[]{:S(2)}) copy-start(f32[4096]{0:T(1024)} %param.9) | copy-start | bytes 49156
  48.1 4.7 %collective-permute-start.1 = (bf16[16,128,128]{2,1,0:T(8,128)(2,1)S(1)}, bf16[16,128,128]{2,1,0:T(8,128)(2,1)S(1)}, u32[]{:S(2)}, u32[]{:S(2)}) collective-permute-start(bf16[16,128,128]{2,1,0:T(8,128)(2,1)S(1)} %shard_map.61), channel_id=1, source_target_pairs={{0,1},{1,0},{2,3},{3,2},{4,5},{5,4},{6,7},{7,6},{8,9},{9,8},{10,11... | collective-permute-start | bytes 1572872 | tf_op jit(solution)/shard_map/ppermute | solution.py:331
  51.1 1.7 %copy-start.2 = (f32[256,2048]{1,0:T(8,128)S(1)}, f32[256,2048]{1,0:T(8,128)}, u32[]{:S(2)}) copy-start(f32[256,2048]{1,0:T(8,128)} %get-tuple-element.28.inner_ref) | copy-start | bytes 6291460

commit v8 on v7

--- a/solution.py
+++ b/solution.py
@@ -19,7 +19,7 @@
 SPLIT = 48
 ROWS = 40
 AHEAD = 1
-READY = 4
+READY = 8
 PART = 4
 MB = 1 << 20
 LIMIT = 12

time: 55.6 us -> 55.6 us (level)
  no operation moved by 1% of the time
where the time goes in v8:
time: 55.6 us; the launch traced here: 55.2 us
  Pallas kernels  18 us (32%)
  starting transfers between devices  15.7 us (28%)
  blocking collectives  15.7 us (28%)
  waiting for transfers between devices  5.69 us (10%)
    all_to_all x1, blocking collectives, on_device(): lax.all_to_all(before, CHIPS, split_axis=0, concat_axis=0, tiled=True)  15.7 us
    all_to_all x1, starting transfers between devices, on_device(): lax.all_to_all(chunks, CHIPS, split_axis=0, concat_axis=0, tiled=True)  11.2 us
    pallas_call x1, Pallas kernels, within_blocks(): pl.pallas_call(within, grid_spec=pltpu.PrefetchScalarGridSpec(num_scalar_...  8.48 us
    all_to_all x1, waiting for transfers between devices, on_device(): lax.all_to_all(chunks, CHIPS, split_axis=0, concat_axis=0, tiled=True)  5.69 us
    ppermute x1, starting transfers between devices, on_device(): taken = swap(give)  3.01 us
    pallas_call x1, Pallas kernels, on_device(): call(finish_other, [smem] + [vmem] * 6, hbm, pltpu.HBM((T, heads * W), BF...  2.42 us
    pallas_call x1, Pallas kernels, on_device(): call(send_states, [smem, hbm, hbm, hbm], vmem, struct((HALF * W + SPLIT,...  2.04 us
    pallas_call x1, Pallas kernels, on_device(): call(own_states, [smem, hbm, hbm, hbm], [vmem, vmem], [struct((HALF, W, W...  2.03 us
  transfers between devices with their start and end apart: 3, of which 1 were waited for; matrix products, arithmetic and copies ran while one was open for 0% of the time, Pallas kernels for 22%

profile of v8, /device:TPU:1, one launch (start us, length us, event | category | flops | bytes accessed | tf_op | source)
XLA Modules:
  0.0 55.2 jit_solution(13350022599411976947)
XLA Ops:
  0.0 2.0 %shard_map.56 = bf16[2096,128]{1,0:T(8,128)(2,1)S(1)} custom-call(s32[1]{0:T(128)} %bitcast.core_ref, bf16[256,4096]{1,0:T(8,128)(2,1)} %k_ref.5, bf16[256,4096]{1,0:T(8,128)(2,1)} %v_ref.5, f32[32,256]{1,0:T(8,128)} %ld_ref.9), custom_call_target="tpu_custom_call" | custom-call | flops 134217728 | bytes 3145728 | tf_op jit(solution)/shard_map/pallas_call | solution.py:307
  2.0 1.5 %collective-permute-start = (bf16[2096,128]{1,0:T(8,128)(2,1)S(1)}, bf16[2096,128]{1,0:T(8,128)(2,1)S(1)}, u32[]{:S(2)}, u32[]{:S(2)}) collective-permute-start(bf16[2096,128]{1,0:T(8,128)(2,1)S(1)} %shard_map.56), channel_id=1, source_target_pairs={{0,1},{1,0},{2,3},{3,2},{4,5},{5,4},{6,7},{7,6},{8,9},{9,8},{10,11... | collective-permute-start | bytes 1609736 | tf_op jit(solution)/shard_map/ppermute | solution.py:311
  3.5 2.0 %shard_map.55 = (f32[16,128,128]{2,1,0:T(8,128)S(1)}, f32[16,128]{1,0:T(8,128)S(1)}) custom-call(s32[1]{0:T(128)} %bitcast.core_ref, bf16[256,4096]{1,0:T(8,128)(2,1)} %k_ref.5, bf16[256,4096]{1,0:T(8,128)(2,1)} %v_ref.5, f32[32,256]{1,0:T(8,128)} %ld_ref.9), custom_call_target="tpu_custom_call" | custom-call | flops 134217728 | bytes 3145728 | tf_op jit(solution)/shard_map/pallas_call | solution.py:312
  5.6 0.0 collective-permute-done.recv_ref
  5.6 1.1 %shard_map.57 = (bf16[64,40,128]{2,1,0:T(8,128)(2,1)}, bf16[16,128,128]{2,1,0:T(8,128)(2,1)S(1)}, f32[16,128]{1,0:T(8,128)S(1)}) custom-call(s32[1]{0:T(128)} %bitcast.core_ref, f32[16,128,128]{2,1,0:T(8,128)S(1)} %get-tuple-element.17.own_ref, f32[16,128]{1,0:T(8,128)S(1)} %get-tuple-element.18.decay_ref, bf16[2096,128]{1,0:T(8,128)(2,1)S(1)} %collective-permute-done.recv_ref), custom_call_target="tpu_custom_call" | custom-call | tf_op jit(solution)/shard_map/pallas_call | solution.py:317
  6.7 11.2 %all-to-all-start = ((bf16[64,40,128]{2,1,0:T(8,128)(2,1)}), bf16[64,40,128]{2,1,0:T(8,128)(2,1)S(1)}, u32[]{:S(2)}, u32[]{:S(2)}) async-start(bf16[64,40,128]{2,1,0:T(8,128)(2,1)} %get-tuple-element.20), calls=%async_computation | async-start | bytes 1310720 | tf_op jit(solution)/shard_map/all_to_all | solution.py:322
  17.9 8.5 %shard_map.58 = (f32[256,2048]{1,0:T(8,128)}, f32[256,2048]{1,0:T(8,128)}) custom-call(s32[1]{0:T(128)} %bitcast.core_ref, f32[32,256]{1,0:T(8,128)} %ld_ref.9, bf16[256,4096]{1,0:T(8,128)(2,1)} %q_ref.4, bf16[256,4096]{1,0:T(8,128)(2,1)} %k_ref.5, bf16[256,4096]{1,0:T(8,128)(2,1)} %v_ref.5), custom_call_target="tpu_custom_call" | custom-call | flops 2147483648 | bytes 10485760 | tf_op jit(solution)/shard_map/pallas_call | solution.py:270
  26.4 0.0 copy-start
  26.4 5.7 %all-to-all-done.in_ref = bf16[64,40,128]{2,1,0:T(8,128)(2,1)S(1)} async-done(((bf16[64,40,128]{2,1,0:T(8,128)(2,1)}), bf16[64,40,128]{2,1,0:T(8,128)(2,1)S(1)}, u32[]{:S(2)}, u32[]{:S(2)}) %all-to-all-start) | async-done | bytes 655392 | tf_op jit(solution)/shard_map/all_to_all | solution.py:322
  32.0 0.2 shard_map.59
  32.2 15.7 %all_to_all.10.chip_ref = bf16[64,32,128]{2,1,0:T(8,128)(2,1)S(1)} all-to-all(bf16[64,32,128]{2,1,0:T(8,128)(2,1)S(1)} %shard_map.59), channel_id=1, replica_groups=mesh['z'=4,'y'=4,'x'=4,'c'=2] {'z','y','x'}, dimensions={0} | all-to-all | bytes 1048576 | tf_op jit(solution)/shard_map/all_to_all | solution.py:326
  47.9 0.0 copy-start.1
  47.9 0.0 copy-start.3
  47.9 0.0 copy-start.4
  47.9 0.0 copy-done
  47.9 0.2 shard_map.61
  48.1 3.0 %collective-permute-start.1 = (bf16[16,128,128]{2,1,0:T(8,128)(2,1)S(1)}, bf16[16,128,128]{2,1,0:T(8,128)(2,1)S(1)}, u32[]{:S(2)}, u32[]{:S(2)}) collective-permute-start(bf16[16,128,128]{2,1,0:T(8,128)(2,1)S(1)} %shard_map.61), channel_id=1, source_target_pairs={{0,1},{1,0},{2,3},{3,2},{4,5},{5,4},{6,7},{7,6},{8,9},{9,8},{10,11... | collective-permute-start | bytes 1572872 | tf_op jit(solution)/shard_map/ppermute | solution.py:331
  51.1 0.0 copy-done.1
  51.1 0.0 copy-done.3
  51.1 0.0 copy-done.4
  51.1 0.0 copy-start.2
  51.1 1.6 %shard_map.60.own_ref = bf16[256,2048]{1,0:T(8,128)(2,1)S(1)} custom-call(s32[1]{0:T(128)} %bitcast.core_ref, f32[32,256]{1,0:T(8,128)S(1)} %copy-done.3, bf16[256,4096]{1,0:T(8,128)(2,1)S(1)} %copy-done.1, f32[256,2048]{1,0:T(8,128)S(1)} %copy-done, bf16[64,32,128]{2,1,0:T(8,128)(2,1)S(1)} %all_to_all.10.chip_ref, ...), custom_call_target="tpu_custom_call" | custom-call | flops 134217728 | bytes 5242880 | tf_op jit(solution)/shard_map/pallas_call | solution.py:333
  52.8 0.0 collective-permute-done.1.carried_ref
  52.8 0.0 copy-done.2
  52.8 2.4 %shard_map.62 = bf16[256,4096]{1,0:T(8,128)(2,1)} custom-call(s32[1]{0:T(128)} %bitcast.core_ref, bf16[256,2048]{1,0:T(8,128)(2,1)S(1)} %shard_map.60.own_ref, f32[32,256]{1,0:T(8,128)S(1)} %copy-done.3, bf16[256,4096]{1,0:T(8,128)(2,1)S(1)} %copy-done.1, f32[256,2048]{1,0:T(8,128)S(1)} %copy-done.2, ...), custom_call_target="tpu_custom_call" | custom-call | flops 134217728 | bytes 5242880 | tf_op jit(solution)/shard_map/pallas_call | solution.py:337
Async XLA Ops:
  2.0 3.5 %collective-permute-start = (bf16[2096,128]{1,0:T(8,128)(2,1)S(1)}, bf16[2096,128]{1,0:T(8,128)(2,1)S(1)}, u32[]{:S(2)}, u32[]{:S(2)}) collective-permute-start(bf16[2096,128]{1,0:T(8,128)(2,1)S(1)} %shard_map.56), channel_id=1, source_target_pairs={{0,1},{1,0},{2,3},{3,2},{4,5},{5,4},{6,7},{7,6},{8,9},{9,8},{10,11... | collective-permute-start | bytes 1609736 | tf_op jit(solution)/shard_map/ppermute | solution.py:311
  6.7 25.4 %all-to-all-start = ((bf16[64,40,128]{2,1,0:T(8,128)(2,1)}), bf16[64,40,128]{2,1,0:T(8,128)(2,1)S(1)}, u32[]{:S(2)}, u32[]{:S(2)}) async-start(bf16[64,40,128]{2,1,0:T(8,128)(2,1)} %get-tuple-element.20), calls=%async_computation | async-start | bytes 1310720 | tf_op jit(solution)/shard_map/all_to_all | solution.py:322
  26.4 21.5 %copy-start = (f32[256,2048]{1,0:T(8,128)S(1)}, f32[256,2048]{1,0:T(8,128)}, u32[]{:S(2)}) copy-start(f32[256,2048]{1,0:T(8,128)} %get-tuple-element.24.inner_ref.near_ref) | copy-start | bytes 6291460
  47.9 3.2 %copy-start.1 = (bf16[256,4096]{1,0:T(8,128)(2,1)S(1)}, bf16[256,4096]{1,0:T(8,128)(2,1)}, u32[]{:S(2)}) copy-start(bf16[256,4096]{1,0:T(8,128)(2,1)} %q_ref.4) | copy-start | bytes 6291460
  47.9 3.2 %copy-start.3 = (f32[32,256]{1,0:T(8,128)S(1)}, f32[32,256]{1,0:T(8,128)}, u32[]{:S(2)}) copy-start(f32[32,256]{1,0:T(8,128)} %ld_ref.9) | copy-start | bytes 98308
  47.9 3.2 %copy-start.4 = (f32[4096]{0:T(1024)S(1)}, f32[4096]{0:T(1024)}, u32[]{:S(2)}) copy-start(f32[4096]{0:T(1024)} %param.9) | copy-start | bytes 49156
  48.1 4.7 %collective-permute-start.1 = (bf16[16,128,128]{2,1,0:T(8,128)(2,1)S(1)}, bf16[16,128,128]{2,1,0:T(8,128)(2,1)S(1)}, u32[]{:S(2)}, u32[]{:S(2)}) collective-permute-start(bf16[16,128,128]{2,1,0:T(8,128)(2,1)S(1)} %shard_map.61), channel_id=1, source_target_pairs={{0,1},{1,0},{2,3},{3,2},{4,5},{5,4},{6,7},{7,6},{8,9},{9,8},{10,11... | collective-permute-start | bytes 1572872 | tf_op jit(solution)/shard_map/ppermute | solution.py:331
  51.1 1.7 %copy-start.2 = (f32[256,2048]{1,0:T(8,128)S(1)}, f32[256,2048]{1,0:T(8,128)}, u32[]{:S(2)}) copy-start(f32[256,2048]{1,0:T(8,128)} %get-tuple-element.28.inner_ref) | copy-start | bytes 6291460
